TPU v7x, 256 devices: a whole 4x4x8 slice. The times are simulated.
256 devices in a mesh: pd: 2 (over core), dp: 4 (over x), ep: 32 (over z, y).
Axes of the slice: x: 4, y: 4, z: 8, core: 2. Of those that a mesh axis runs over, the one named last changes fastest.
Arguments:
- queries: bfloat16 [512, 64, 576], P(('pd', 'dp', 'ep')), may hold values from -270 to 270
- cache_vals: bfloat16 [256, 1024, 576], P(('pd', 'dp', 'ep')), may hold values from -6 to 6
- cache_scales: bfloat16 [256, 4, 1024], P(('pd', 'dp', 'ep')), may hold values from 0.25 to 2, as said below
- cache_len: int32 [256], P(('pd', 'dp', 'ep')), may hold values from 256 to 1024, as said below
- fresh_vals: bfloat16 [256, 1024, 576], P(('pd', 'dp', 'ep')), may hold values from -6 to 6
- fresh_scales: bfloat16 [256, 4, 1024], P(('pd', 'dp', 'ep')), may hold values from 0.25 to 2, as said below
- fresh_len: int32 [256], P(('pd', 'dp', 'ep')), may hold values from 512 to 1024, as said below
- fresh_owner: int32 [256], P(('pd', 'dp', 'ep')), may hold values from 0 to 3, as said below
- hidden: bfloat16 [512, 7168], P(('pd', 'dp', 'ep')), may hold values from -4 to 4
- w_uv: bfloat16 [64, 512, 128], P(('pd', 'ep')), may hold values from -1 to 1
- w_out: bfloat16 [8192, 7168], P(('pd', 'ep')), may hold values from -0.0625 to 0.0625
- norm_gain: bfloat16 [7168], replicated, may hold values from 0.5 to 1.5
- route_ids: int32 [512, 8], replicated, may hold values from 0 to 31, all different within a row; in each aligned block of 64 rows (0 to 63, 64 to 127, ...) at most 32 rows name the same one
- route_weights: float32 [512, 8], replicated, may hold values from 0.05 to 0.5
- w_gate: bfloat16 [32, 7168, 1024], P('ep', None, ('pd', 'dp')), may hold values from -0.0625 to 0.0625
- w_up: bfloat16 [32, 7168, 1024], P('ep', None, ('pd', 'dp')), may hold values from -0.0625 to 0.0625
- w_down: bfloat16 [32, 1024, 7168], P('ep', ('pd', 'dp')), may hold values from -0.1875 to 0.1875
Outputs:
- layer_out: bfloat16 [512, 7168], P(('pd', 'dp', 'ep'))
Inputs may be any that keep to these rules, and one draw needn't show every extreme that they name: `cache_scales`: every entry is a power of two. `fresh_scales`: every entry is a power of two. `cache_len`: some old request has all 1024 tokens valid. `fresh_len`: some new request has all 1024 tokens valid. For each p < 2 and e < 32, the entries fresh_owner[(p * 4 + i) * 32 + e] over i < 4 take every index along dp exactly once. `route_ids`: each row names 8 different experts. In each aligned block of 64 rows no expert is named by more than 32 rows, a bound that some block reaches.
All inputs are finite; a program needn't handle non-finite values.
Results may differ from a plain program's by a relative error of at most 0.013.
Values may be sent and summed in bfloat16 or wider, within the bound.
No kernel may reach another device: no remote copies, remote signals or barrier semaphores. Data moves between devices by JAX's collectives and lax.ppermute only.
A program may use at most 64 MiB of HBM per device.

v0:
```python
import functools

import jax
import jax.numpy as jnp
import numpy as np
from jax import lax
from jax.experimental import pallas as pl
from jax.experimental.pallas import tpu as pltpu
from jax.sharding import PartitionSpec as P

DLAT = 512
CHIPS_Y = 4


SOFT_SCALE = 0.07216878364870323
EPSILON = 1e-06
BF16 = jnp.bfloat16
F32 = jnp.float32


def shift(value, axis, amount):
    size = lax.axis_size(axis)
    return lax.ppermute(value, axis, [(i, (i + amount) % size) for i in range(size)])


def exchange(value, axis, groups=None):
    return lax.all_to_all(value, axis, 0, 0, axis_index_groups=groups)


def dot(left, right):
    return jnp.dot(left, right, preferred_element_type=F32)


HIGHEST = lax.Precision.HIGHEST
VMEM = pl.BlockSpec(memory_space=pltpu.VMEM)
SMEM = pl.BlockSpec(memory_space=pltpu.SMEM)
HBM = pl.BlockSpec(memory_space=pltpu.HBM)
ANY = pl.BlockSpec(memory_space=pl.ANY)
PARAMS = pltpu.CompilerParams(vmem_limit_bytes=16 * 1024 * 1024)
WIDE = pltpu.CompilerParams(vmem_limit_bytes=58 * 1024 * 1024)


def shape(dims, dtype):
    return jax.ShapeDtypeStruct(dims, dtype)


def attend(query, keys_ref, scales_ref, length, held_ref):
    for block in range(scales_ref.shape[0]):
        at = slice(block * 128, block * 128 + 128)
        scale = scales_ref[...].astype(F32)[block : block + 1]
        held_ref[at] = (keys_ref[at].astype(F32) * scale).astype(BF16)
    scores = dot(query[:, :DLAT], held_ref[...]) + dot(query[:, DLAT:], keys_ref[DLAT:])
    scores = scores * SOFT_SCALE
    token = lax.broadcasted_iota(jnp.int32, scores.shape, 1)
    scores = jnp.where(token < length, scores, -1e30)
    weights = jnp.exp(scores - jnp.max(scores, axis=1, keepdims=True))
    probs = (weights / jnp.sum(weights, axis=1, keepdims=True)).astype(BF16)
    return lax.dot_general(
        probs, held_ref[...], (((1,), (1,)), ((), ())), preferred_element_type=F32
    )


def parcel_kernel(lines, at_ref, owner_ref, query_ref, hidden_ref, *outs):
    heads, wide = query_ref.shape[1:]
    cols = hidden_ref.shape[1] // lines
    lanes = outs[0].shape[1]
    for s in range(lines):
        start = pl.multiple_of(lax.rem(at_ref[0] + s, lines) * cols, 128)
        hidden = hidden_ref[:, pl.ds(start, cols)].astype(F32)
        parts = [hidden[:, at : at + lanes] for at in range(0, cols, lanes)]
        parts = [jnp.pad(part, ((0, 0), (0, lanes - part.shape[1]))) for part in parts]
        used = 2 * len(parts)
        parts.append(jnp.full((16 - used, lanes), owner_ref[0].astype(F32)))
        outs[s][:heads, :wide] = query_ref[1]
        outs[s][:heads, wide:] = jnp.zeros((heads, lanes - wide), BF16)
        outs[s][heads:] = jnp.concatenate(parts, axis=0).astype(BF16)


def make_parcels(dp, lines, owner, query, hidden):
    out = shape((query.shape[1] + 16, -(-query.shape[2] // 128) * 128), BF16)
    return pl.pallas_call(
        functools.partial(parcel_kernel, lines),
        out_shape=[out] * lines,
        in_specs=[SMEM, SMEM, VMEM, VMEM],
        out_specs=[VMEM] * lines,
        compiler_params=PARAMS,
    )(dp, owner, query, hidden)


def mask_kernel(sizes, at_ref, ids_ref, gates_ref, before_ref, there_ref, back_ref, *outs):
    chips_y, chips_z, lines, capacity = sizes
    select_ref, table_ref, gate_ref, line_ref = outs
    expert, place_z = at_ref[1], at_ref[3]
    rows, slots = ids_ref.shape[1], lines * capacity
    hits = ids_ref[...] == expert
    routed = jnp.sum(jnp.where(hits, 1.0, 0.0), axis=0, keepdims=True)
    gates = jnp.sum(jnp.where(hits, gates_ref[...], 0.0), axis=0, keepdims=True)
    place = dot(jnp.broadcast_to(routed, (8, rows)).astype(BF16), before_ref[...])[:1]
    lane = lax.broadcasted_iota(jnp.int32, (1, rows), 1)
    first = lax.div(lane, rows // lines) * capacity
    slot = jnp.where(routed > 0.0, place + first.astype(F32), -1.0)
    wide = jnp.broadcast_to(slot, (8, rows)).astype(BF16)
    slot_iota = lax.broadcasted_iota(jnp.int32, (slots, rows), 0).astype(F32)
    select_ref[...] = jnp.where(dot(wide, there_ref[...])[:1] == slot_iota, 1.0, 0.0).astype(BF16)
    back = jnp.where(dot(wide, back_ref[...])[:1] == slot_iota, 1.0, 0.0)
    table_ref[...] = back.T.astype(BF16)
    gate_ref[...] = jnp.sum(jnp.where(slot == slot_iota, gates, 0.0), axis=1, keepdims=True)
    pairs = 2 * chips_z
    out = lax.broadcasted_iota(jnp.int32, line_ref.shape, 0)
    come = lax.broadcasted_iota(jnp.int32, line_ref.shape, 1)
    own = lax.rem(lax.div(out, 2), chips_z) == place_z
    own = own & (lax.div(out, pairs) * 2 + lax.rem(out, 2) == come)
    line_ref[...] = jnp.where(own, 1.0, 0.0)


def make_masks(at, sizes, ids, gates):
    chips_y, chips_z, lines, capacity = sizes
    rows, slots, pairs = ids.shape[1], lines * capacity, 2 * chips_z
    canon = np.arange(rows).reshape(lines, chips_z, chips_y, 2)
    eye = np.eye(rows)
    before = np.kron(np.eye(lines), np.triu(np.ones((rows // lines, rows // lines)), 1))
    there = eye[canon.transpose(2, 1, 0, 3).reshape(rows)].T
    back = eye[canon.transpose(2, 0, 1, 3).reshape(rows)].T
    return pl.pallas_call(
        functools.partial(mask_kernel, sizes),
        out_shape=[
            shape((slots, rows), BF16),
            shape((rows, slots), BF16),
            shape((slots, 1), F32),
            shape((lines * pairs, 2 * lines), F32),
        ],
        in_specs=[SMEM] + [VMEM] * 5,
        out_specs=[VMEM] * 4,
        compiler_params=PARAMS,
    )(at, ids, gates, *(jnp.asarray(m, BF16) for m in (before, there, back)))


def old_kernel(lines, at_ref, len_ref, query_ref, order_ref, keys_ref, scales_ref, *rest):
    gate_ref, up_ref, down_ref, out_ref = rest[:4]
    outs, held_ref, sems = rest[4:-2], rest[-2], rest[-1]
    cols, units = outs[1].shape[1], gate_ref.shape[1]
    copies = []
    for s in range(lines):
        start = pl.multiple_of(lax.rem(at_ref[0] + s, lines) * cols, 128)
        both, down = outs[2 * s], outs[2 * s + 1]
        copies.append((gate_ref.at[pl.ds(start, cols)], both.at[:, pl.ds(0, units)]))
        copies.append((up_ref.at[pl.ds(start, cols)], both.at[:, pl.ds(units, units)]))
        copies.append((down_ref.at[:, pl.ds(start, cols)], down))
    copies = [pltpu.make_async_copy(a, b, sems.at[i]) for i, (a, b) in enumerate(copies)]
    for copy in copies:
        copy.start()
    query = dot(order_ref[...], query_ref[0]).astype(BF16)
    result = attend(query, keys_ref, scales_ref, len_ref[0], held_ref)
    rows = out_ref.shape[1]
    for z in range(out_ref.shape[0]):
        out_ref[z] = result[z * rows : (z + 1) * rows].astype(BF16)
    for copy in copies:
        copy.wait()


def old_attention(dp, lines, length, query, order, keys, scales, gate, up, down, pieces):
    cols, units = gate.shape[0] // lines, gate.shape[1]
    rows = query.shape[1] // pieces
    return pl.pallas_call(
        functools.partial(old_kernel, lines),
        out_shape=[shape((pieces, rows, DLAT), BF16)]
        + [shape((cols, 2 * units), BF16), shape((units, cols), BF16)] * lines,
        in_specs=[SMEM, SMEM] + [VMEM] * 4 + [HBM] * 3,
        out_specs=[VMEM] * (2 * lines + 1),
        scratch_shapes=[
            pltpu.VMEM((DLAT, keys.shape[1]), BF16),
            pltpu.SemaphoreType.DMA((3 * lines,)),
        ],
        compiler_params=WIDE,
        cost_estimate=pl.CostEstimate(
            flops=2 * query.size * keys.shape[1],
            bytes_accessed=2 * (keys.size + 2 * (gate.size + up.size + down.size)),
            transcendentals=query.shape[1] * keys.shape[1],
        ),
    )(dp, length, query, order, keys, scales, gate, up, down)


def new_kernel(lines, step_ref, len_ref, order_ref, keys_ref, scales_ref, old_ref, *rest):
    parcel_refs, out_ref, held_ref = rest[:lines], rest[lines], rest[lines + 1]
    heads, width = order_ref.shape[0], keys_ref.shape[0]
    query = parcel_refs[0][:heads, :width]
    for s in range(1, lines):
        query = jnp.where(step_ref[0] == s, parcel_refs[s][:heads, :width], query)
    query = dot(order_ref[...], query).astype(BF16)
    result = attend(query, keys_ref, scales_ref, len_ref[0], held_ref)
    rows = out_ref.shape[2]
    for z in range(out_ref.shape[0]):
        out_ref[z, 0] = old_ref[z]
        out_ref[z, 1] = result[z * rows : (z + 1) * rows].astype(BF16)


def new_attention(step, length, order, keys, scales, old, parcels):
    return pl.pallas_call(
        functools.partial(new_kernel, len(parcels)),
        out_shape=shape((old.shape[0], 2) + old.shape[1:], BF16),
        in_specs=[SMEM, SMEM] + [VMEM] * (4 + len(parcels)),
        out_specs=VMEM,
        scratch_shapes=[pltpu.VMEM((DLAT, keys.shape[1]), BF16)],
        compiler_params=PARAMS,
    )(step, length, order, keys, scales, old, *parcels)


def sort_kernel(chips_y, at_ref, rows_ref, own_ref, other_ref):
    half = own_ref.shape[0]
    pairs = half // chips_y
    core, place_y = at_ref[0], at_ref[2]
    out = lax.broadcasted_iota(jnp.int32, (2 * half, 2 * half), 0)
    want = lax.div(out, half)
    want = jnp.where(want == 0, core, 1 - core)
    turn = lax.rem(place_y - lax.rem(lax.div(out, pairs), chips_y) + chips_y, chips_y)
    want = lax.rem(out, pairs) * (2 * chips_y) + want * chips_y + turn
    come = lax.broadcasted_iota(jnp.int32, (2 * half, 2 * half), 1)
    order = jnp.where(want == come, 1.0, 0.0).astype(BF16)
    result = dot(order, rows_ref[...]).astype(BF16)
    own_ref[...] = result[:half]
    other_ref[...] = result[half:]


def sort_rows(at, chips_y, rows):
    half = shape((rows.shape[0] // 2, rows.shape[1]), BF16)
    return pl.pallas_call(
        functools.partial(sort_kernel, chips_y),
        out_shape=[half, half],
        in_specs=[SMEM, VMEM],
        out_specs=[VMEM, VMEM],
        compiler_params=PARAMS,
    )(at, rows)


def values_kernel(own_ref, other_ref, uv_ref, out_ref):
    count, _, width = uv_ref.shape
    rows = own_ref.shape[0] // count
    for s in range(count):
        for q, ref in enumerate((own_ref, other_ref)):
            result = dot(ref[s * rows : (s + 1) * rows], uv_ref[s]).astype(BF16)
            for i in range(out_ref.shape[0]):
                out_ref[i, q * rows : (q + 1) * rows, s * width : (s + 1) * width] = result


def head_values(lines, own, other, uv_all):
    count, _, width = uv_all.shape
    return pl.pallas_call(
        values_kernel,
        out_shape=shape((lines, 2 * own.shape[0] // count, count * width), BF16),
        in_specs=[VMEM] * 3,
        out_specs=VMEM,
        compiler_params=PARAMS,
    )(own, other, uv_all)


def project_kernel(values_ref, order_ref, *rest):
    out_refs, own_ref, other_ref = rest[:-2], rest[-2], rest[-1]
    rows = values_ref.shape[0] // 2
    values = dot(order_ref[...], values_ref[...]).astype(BF16)
    width = out_refs[0].shape[0]
    for start in range(0, own_ref.shape[1], 256):
        total = sum(
            dot(values[:, s * width : (s + 1) * width], ref[:, start : start + 256])
            for s, ref in enumerate(out_refs)
        )
        own_ref[:, start : start + 256] = total[:rows]
        other_ref[:, start : start + 256] = total[rows:].astype(BF16)


def project(values, order, out_parts):
    rows, cols = values.shape[0] // 2, out_parts[0].shape[1]
    return pl.pallas_call(
        project_kernel,
        out_shape=[shape((rows, cols), F32), shape((rows, cols), BF16)],
        in_specs=[VMEM] * (2 + len(out_parts)),
        out_specs=[VMEM, VMEM],
        compiler_params=PARAMS,
    )(values, order, *out_parts)


def line_kernel(heads, at_ref, gain_ref, *rest):
    parcel_refs, out_ref = rest[:-1], rest[-1]
    lines, cols = len(parcel_refs), gain_ref.shape[1]
    row = lax.broadcasted_iota(jnp.int32, (2 * lines, 128), 0)
    come = lax.broadcasted_iota(jnp.int32, (2 * lines, 128), 1)
    same = lax.rem(row, 2) == lax.rem(come, 2)
    old = lax.rem(row, 2) == 0
    row, come = lax.div(row, 2), lax.div(come, 2)
    order = jnp.where(same & old & (row == come), 1.0, 0.0)
    turned = jnp.zeros_like(order)
    hidden = []
    for s, ref in enumerate(parcel_refs):
        source = lax.rem(at_ref[0] - s + lines, lines)
        lower = ref[heads:].astype(F32)
        lanes = lower.shape[1]
        count = -(-cols // lanes)
        owner = lower[2 * count : 2 * count + 1, :1]
        moved = same & ~old & (come == source) & (row.astype(F32) == owner)
        order = order + jnp.where(moved, 1.0, 0.0)
        turned = turned + jnp.where(same & (come == s) & (row == source), 1.0, 0.0)
        pieces = [
            lower[2 * j : 2 * j + 2, : min(lanes, cols - j * lanes)] for j in range(count)
        ]
        hidden.append(jnp.concatenate(pieces, axis=1))
    hidden = jnp.concatenate(hidden, axis=0)
    rows = 2 * lines
    out_ref[:rows] = jnp.dot(
        turned[:, :rows], hidden, precision=HIGHEST, preferred_element_type=F32
    )
    out_ref[rows : 2 * rows] = jnp.broadcast_to(gain_ref[...].astype(F32), (rows, cols))
    out_ref[2 * rows :, :128] = order
    out_ref[2 * rows :, 128:] = jnp.zeros((rows, cols - 128), F32)


def line_rows(dp, heads, gain, parcels):
    return pl.pallas_call(
        functools.partial(line_kernel, heads),
        out_shape=shape((6 * len(parcels), gain.shape[1]), F32),
        in_specs=[SMEM] + [VMEM] * (1 + len(parcels)),
        out_specs=VMEM,
        compiler_params=PARAMS,
    )(dp, gain, *parcels)


def residual_kernel(sums_ref, line_ref, resid_ref, parcel_ref):
    rows, cols = resid_ref.shape
    total = sums_ref[0].astype(F32)
    for i in range(1, sums_ref.shape[0]):
        total = total + sums_ref[i].astype(F32)
    order = line_ref[2 * rows :, :128][:, :rows]
    resid = jnp.dot(order, total, precision=HIGHEST, preferred_element_type=F32)
    resid = resid + line_ref[:rows]
    resid_ref[...] = resid
    squares = jnp.sum(resid * resid, axis=1, keepdims=True)
    high = squares.astype(BF16)
    low = (squares - high.astype(F32)).astype(BF16)
    lanes = lax.broadcasted_iota(jnp.int32, (rows, 128), 1)
    beside = jnp.where(lanes < 64, high.astype(F32), low.astype(F32)).astype(BF16)
    parcel = (resid * line_ref[rows : 2 * rows]).astype(BF16)
    for i in range(parcel_ref.shape[0]):
        parcel_ref[i, :, :cols] = parcel
        parcel_ref[i, :, cols:] = beside


def residual(sums, line):
    copies, rows, cols = sums.shape
    return pl.pallas_call(
        residual_kernel,
        out_shape=[shape((rows, cols), F32), shape((copies, rows, cols + 128), BF16)],
        in_specs=[VMEM, VMEM],
        out_specs=[VMEM, VMEM],
        compiler_params=PARAMS,
    )(sums, line)


def select_kernel(at_ref, select_ref, *rest):
    columns, out_ref, held_ref = rest[:-2], rest[-2], rest[-1]
    count, rows = len(columns), columns[0].shape[0]
    for s, ref in enumerate(columns):
        held_ref[lax.rem(at_ref[2] - s + count, count)] = ref[...]
    for at in range(0, out_ref.shape[1], 384):
        lanes = slice(at, min(at + 384, out_ref.shape[1]))
        gathered = held_ref[:, :, lanes].reshape(count * rows, lanes.stop - at)
        out_ref[:, lanes] = dot(select_ref[...], gathered).astype(BF16)


def select_rows(at, select, columns):
    return pl.pallas_call(
        select_kernel,
        out_shape=shape((select.shape[0], columns[0].shape[1]), BF16),
        in_specs=[SMEM] + [VMEM] * (1 + len(columns)),
        out_specs=VMEM,
        scratch_shapes=[pltpu.VMEM((len(columns),) + columns[0].shape, BF16)],
        compiler_params=PARAMS,
    )(at, select, *columns)


def acts_kernel(width, units, sums_ref, out_ref):
    total = sums_ref[0].astype(F32)
    for i in range(1, sums_ref.shape[0]):
        total = total + sums_ref[i].astype(F32)
    end = sums_ref.shape[2] - 128
    squares = total[:, end : end + 1] + total[:, end + 64 : end + 65]
    scale = lax.rsqrt(squares / width + EPSILON)
    for j in range(end // (2 * units)):
        at = 2 * units * j
        gate = total[:, at : at + units] * scale
        up = total[:, at + units : at + 2 * units] * scale
        acts = (gate / (1.0 + jnp.exp(-gate)) * up).astype(BF16)
        for i in range(out_ref.shape[0]):
            out_ref[i, :, j * units : (j + 1) * units] = acts


def activations(width, units, sums):
    lines, rows, lanes = sums.shape
    return pl.pallas_call(
        functools.partial(acts_kernel, width, units),
        out_shape=shape((lines, rows, (lanes - 128) // 2), BF16),
        in_specs=[VMEM],
        out_specs=VMEM,
        compiler_params=PARAMS,
    )(sums)


def gate_up_kernel(lines, at_ref, own_ref, other_ref, *rest):
    parts, out_ref, held, sems = rest[:-3], rest[-3], rest[-2], rest[-1]
    cols, lanes = held.shape[1:]
    copies = [pltpu.make_async_copy(parts[s], held.at[s], sems.at[s]) for s in range(lines)]
    for copy in copies:
        copy.start()
    for s in range(lines):
        copies[s].wait()
        lane = pl.multiple_of(lax.rem(at_ref[0] - s + lines, lines) * lanes, 128)
        for q, ref in enumerate((own_ref, other_ref)):
            capacity = ref.shape[0] // lines
            result = dot(ref[:, :cols], held[s]).astype(BF16)
            for d in range(lines):
                out_ref[d, q * capacity : (q + 1) * capacity, pl.ds(lane, lanes)] = result[
                    d * capacity : (d + 1) * capacity
                ]
    for q, ref in enumerate((own_ref, other_ref)):
        capacity = ref.shape[0] // lines
        for d in range(lines):
            out_ref[d, q * capacity : (q + 1) * capacity, lines * lanes :] = ref[
                d * capacity : (d + 1) * capacity, cols:
            ]


def gate_up(dp, own, other, parts):
    lines, (cols, lanes) = len(parts), parts[0].shape
    return pl.pallas_call(
        functools.partial(gate_up_kernel, lines),
        out_shape=shape((lines, 2 * own.shape[0] // lines, lines * lanes + 128), BF16),
        in_specs=[SMEM, VMEM, VMEM] + [ANY] * lines,
        out_specs=VMEM,
        scratch_shapes=[
            pltpu.VMEM((lines, cols, lanes), BF16),
            pltpu.SemaphoreType.DMA((lines,)),
        ],
        compiler_params=PARAMS,
    )(dp, own, other, *parts)


def down_kernel(lines, at_ref, acts_ref, *rest):
    parts, own_ref, other_ref, held, sems = rest[:-4], rest[-4], rest[-3], rest[-2], rest[-1]
    units, cols = parts[0].shape
    copies = []
    for s in range(lines):
        row = pl.multiple_of(lax.rem(at_ref[0] - s + lines, lines) * units, 128)
        copies.append(pltpu.make_async_copy(parts[s], held.at[pl.ds(row, units)], sems.at[s]))
    for copy in copies:
        copy.start()
    for copy in copies:
        copy.wait()
    capacity = acts_ref.shape[1] // 2
    own = jnp.concatenate([acts_ref[d, :capacity] for d in range(lines)], axis=0)
    other = jnp.concatenate([acts_ref[d, capacity:] for d in range(lines)], axis=0)
    for at in range(0, cols, 256):
        own_ref[:, at : at + 256] = dot(own, held[:, at : at + 256])
        other_ref[:, at : at + 256] = dot(other, held[:, at : at + 256]).astype(BF16)


def down(dp, acts, parts):
    lines, (units, cols) = len(parts), parts[0].shape
    slots = acts.shape[0] * acts.shape[1] // 2
    return pl.pallas_call(
        functools.partial(down_kernel, lines),
        out_shape=[shape((slots, cols), F32), shape((slots, cols), BF16)],
        in_specs=[SMEM, VMEM] + [ANY] * lines,
        out_specs=[VMEM, VMEM],
        scratch_shapes=[
            pltpu.VMEM((lines * units, cols), BF16),
            pltpu.SemaphoreType.DMA((lines,)),
        ],
        compiler_params=PARAMS,
    )(dp, acts, *parts)


def expand_kernel(own_ref, other_ref, gate_ref, select_ref, out_ref):
    for at in range(0, own_ref.shape[1], 256):
        total = own_ref[:, at : at + 256] + other_ref[:, at : at + 256].astype(F32)
        weighted = (total * gate_ref[...]).astype(BF16)
        out_ref[:, at : at + 256] = dot(select_ref[...], weighted).astype(BF16)


def expand(own, other, gates, select):
    return pl.pallas_call(
        expand_kernel,
        out_shape=shape((select.shape[0], own.shape[1]), BF16),
        in_specs=[VMEM] * 4,
        out_specs=VMEM,
        compiler_params=PARAMS,
    )(own, other, gates, select)


def join_kernel(line_ref, resid_ref, *rest):
    parts, out_ref = rest[:-1], rest[-1]
    total = jnp.dot(
        line_ref[...], resid_ref[...], precision=HIGHEST, preferred_element_type=F32
    )
    for part in parts:
        total = total + part[...].astype(F32)
    out_ref[...] = total.astype(BF16)


def join(line, resid, parts):
    return pl.pallas_call(
        join_kernel,
        out_shape=shape(parts[0].shape, BF16),
        in_specs=[VMEM] * (2 + len(parts)),
        out_specs=VMEM,
        compiler_params=PARAMS,
    )(line, resid, *parts)


def shards(
    queries,
    cache_vals,
    cache_scales,
    cache_len,
    fresh_vals,
    fresh_scales,
    fresh_len,
    fresh_owner,
    hidden,
    w_uv,
    w_out,
    norm_gain,
    route_ids,
    route_weights,
    w_gate,
    w_up,
    w_down,
):
    pd, dp, ep = lax.axis_index("pd"), lax.axis_index("dp"), lax.axis_index("ep")
    n_pd, n_dp, n_ep = lax.axis_size("pd"), lax.axis_size("dp"), lax.axis_size("ep")
    heads, key_width = queries.shape[1:]
    width = hidden.shape[1]
    cols = width // n_dp
    units = w_gate.shape[2]

    chips_y = CHIPS_Y
    chips_z = n_ep // chips_y
    z_groups = [[z * chips_y + y for z in range(chips_z)] for y in range(chips_y)]
    place_y = ep % chips_y

    def shift_y(value, amount):
        pairs = [
            (z * chips_y + y, z * chips_y + (y + amount) % chips_y)
            for z in range(chips_z)
            for y in range(chips_y)
        ]
        return lax.ppermute(value, "ep", pairs)

    at_dp = dp.astype(jnp.int32).reshape(1)
    parcels = make_parcels(at_dp, n_dp, fresh_owner, queries, hidden)
    parcels = list(parcels[:1]) + [shift(parcels[s], "dp", s) for s in range(1, n_dp)]
    gain = lax.dynamic_slice_in_dim(norm_gain, dp * cols, cols, 0)[None]

    whole, first = lax.optimization_barrier((queries, parcels[1]))

    order = np.arange(heads).reshape(n_pd, chips_z, chips_y).transpose(1, 0, 2).reshape(heads)
    order = jnp.asarray(np.eye(heads)[order], BF16)
    packed = old_attention(
        at_dp,
        n_dp,
        cache_len,
        whole,
        order,
        cache_vals[0].T,
        cache_scales[0],
        w_gate[0],
        w_up[0],
        w_down[0],
        chips_z,
    )
    old_out, packed = packed[0], packed[1:]
    uv_own = w_uv[0]
    out_own = lax.dynamic_slice_in_dim(w_out, dp * cols, cols, 1)
    uv_parts = [uv_own] + [shift_y(uv_own, s) for s in range(1, chips_y)]
    out_parts = [out_own] + [shift_y(out_own, s) for s in range(1, chips_y)]
    old_out, rest, uv_parts = lax.optimization_barrier((old_out, parcels[2:], uv_parts))
    parcels = [parcels[0], first] + list(rest)
    parcels, packed = lax.optimization_barrier((parcels, packed))
    both_parts = [packed[0]] + [shift(packed[2 * s], "dp", s) for s in range(1, n_dp)]
    down_parts = [packed[1]] + [shift(packed[2 * s + 1], "dp", s) for s in range(1, n_dp)]
    step = (dp - fresh_owner) % n_dp
    latent = new_attention(
        step, fresh_len, order, fresh_vals[0].T, fresh_scales[0], old_out, parcels
    )
    slab = 2 * n_ep
    capacity = 2 * slab * route_ids.shape[1] // n_ep
    latent, ids, gates, parcels = lax.optimization_barrier(
        (latent, route_ids.T, route_weights.T, parcels)
    )
    at = jnp.stack([pd, ep, place_y, ep // chips_y]).astype(jnp.int32)
    masks = make_masks(
        at,
        (chips_y, chips_z, n_dp, capacity),
        lax.dynamic_slice_in_dim(ids, pd * n_dp * slab, n_dp * slab, 1),
        lax.dynamic_slice_in_dim(gates, pd * n_dp * slab, n_dp * slab, 1),
    )
    head_rows = exchange(latent, "ep", z_groups)
    line = line_rows(at_dp, heads, gain, parcels)
    head_rows, near, uv_all, masks, line = lax.optimization_barrier(
        (head_rows, out_parts[1::2], jnp.stack(uv_parts), masks, line)
    )
    select, select_back, slot_gate, own_line = masks
    own, other = sort_rows(at, chips_y, head_rows.reshape(2 * chips_z * heads // chips_z, DLAT))
    values = head_values(n_dp, own, shift(other, "pd", 1), uv_all)
    values, far = lax.optimization_barrier((values, out_parts[2]))
    out_parts = [out_own, near[0], far, near[1]]
    values = exchange(values, "dp")
    values, near = lax.optimization_barrier((values, both_parts[1::2]))
    rows = n_dp * 2 * chips_z * 2
    order = np.arange(rows).reshape(n_dp, 2, chips_z, 2).transpose(1, 2, 0, 3).reshape(rows)
    order = jnp.asarray(np.eye(rows)[order], BF16)
    own, other = project(values.reshape(rows, chips_y * 128), order, out_parts)
    partial = (own + shift(other, "pd", 1).astype(F32)).astype(BF16)
    summands = exchange(partial.reshape(chips_z, n_dp * 2, cols), "ep", z_groups)
    resid_cols, parcel = residual(summands, line)
    column = exchange(parcel, "ep", z_groups)
    column, far = lax.optimization_barrier((column, both_parts[2]))
    both_parts = [both_parts[0], near[0], far, near[1]]
    column = column.reshape(chips_z * n_dp * 2, cols + 128)
    columns = [column] + [shift_y(column, s) for s in range(1, chips_y)]
    columns, down_parts = lax.optimization_barrier((columns, down_parts))
    slot_rows = select_rows(at, select, columns)
    other_rows = shift(slot_rows, "pd", 1)

    halves = gate_up(at_dp, slot_rows, other_rows, both_parts)
    all_acts = exchange(activations(width, units, exchange(halves, "dp")), "dp")
    own, other = down(at_dp, all_acts, down_parts)
    table = expand(own, shift(other, "pd", 1), slot_gate, select_back)
    table = table.reshape(chips_y, n_dp * chips_z * 2, cols)
    parts = [lax.dynamic_index_in_dim(table, place_y, 0, keepdims=False)]
    for s in range(1, chips_y):
        part = lax.dynamic_index_in_dim(table, (place_y + s) % chips_y, 0, keepdims=False)
        parts.append(shift_y(part, s))
    table = join(own_line, resid_cols, parts).reshape(n_dp * chips_z, 2, cols)
    planes = [
        [d * n_ep + z * chips_y + y for d in range(n_dp) for z in range(chips_z)]
        for y in range(chips_y)
    ]
    table = exchange(table, ("dp", "ep"), planes).reshape(n_dp, chips_z, 2, cols)
    out = jnp.sum(table.astype(F32), axis=1).astype(BF16)
    return out.transpose(1, 0, 2).reshape(2, width)


def solution(mesh):
    in_specs = (
        P(("pd", "dp", "ep"), None, None),
        P(("pd", "dp", "ep"), None, None),
        P(("pd", "dp", "ep"), None, None),
        P(("pd", "dp", "ep")),
        P(("pd", "dp", "ep"), None, None),
        P(("pd", "dp", "ep"), None, None),
        P(("pd", "dp", "ep")),
        P(("pd", "dp", "ep")),
        P(("pd", "dp", "ep"), None),
        P(("pd", "ep"), None, None),
        P(("pd", "ep"), None),
        P(),
        P(),
        P(),
        P("ep", None, ("pd", "dp")),
        P("ep", None, ("pd", "dp")),
        P("ep", ("pd", "dp"), None),
    )
    out_specs = P(("pd", "dp", "ep"), None)
    return jax.shard_map(shards, mesh=mesh, in_specs=in_specs, out_specs=out_specs, check_vma=False)
```

profile of v0, /device:TPU:24, one launch (start us, length us, event | category | flops | bytes accessed | tf_op | source)
XLA Modules:
  0.0 181.3 jit_solution(5677734037080453093)
XLA Ops:
  4.6 2.3 %collective-permute-start.4 = (bf16[512,128]{1,0:T(8,128)(2,1)}, bf16[512,128]{1,0:T(8,128)(2,1)}, u32[]{:S(2)}, u32[]{:S(2)}) collective-permute-start(bf16[512,128]{1,0:T(8,128)(2,1)} %bitcast.56), channel_id=1, source_target_pairs={{0,2},{1,3},{2,0},{3,1},{4,6},{5,7},{6,4},{7,5},{8,10},{9,11},{10,... | collective-permute-start | bytes 393224 | tf_op jit(solution)/shard_map/ppermute | solution.py:553
  6.9 2.7 %collective-permute-start.1 = (bf16[80,640]{1,0:T(8,128)(2,1)S(1)}, bf16[80,640]{1,0:T(8,128)(2,1)S(1)}, u32[]{:S(2)}, u32[]{:S(2)}) collective-permute-start(bf16[80,640]{1,0:T(8,128)(2,1)S(1)} %get-tuple-element.85), channel_id=1, source_target_pairs={{0,64},{32,96},{64,0},{96,32},{1,65},{33,97},{65,1},{97,33},{2,66}... | collective-permute-start | bytes 307208 | tf_op jit(solution)/shard_map/ppermute | solution.py:23
  11.7 6.7 %shard_map.209 = (bf16[8,8,512]{2,1,0:T(8,128)(2,1)}, bf16[1792,256]{1,0:T(8,128)(2,1)}, bf16[128,1792]{1,0:T(8,128)(2,1)}, bf16[1792,256]{1,0:T(8,128)(2,1)}, b...) custom-call(s32[1]{0:T(128)} %bitcast.at_ref, ...), custom_call_target="tpu_custom_call" | custom-call | flops 150994944 | bytes 12189696 | tf_op jit(solution)/shard_map/pallas_call | solution.py:164
  19.1 2.6 %collective-permute-start.11 = (bf16[1792,256]{1,0:T(8,128)(2,1)}, bf16[1792,256]{1,0:T(8,128)(2,1)}, u32[]{:S(2)}, u32[]{:S(2)}) collective-permute-start(bf16[1792,256]{1,0:T(8,128)(2,1)} %get-tuple-element.126), channel_id=1, source_target_pairs={{0,96},{32,0},{64,32},{96,64},{1,97},{33,1},{65,33},{97,65},{2,98}... | collective-permute-start | bytes 2752520 | tf_op jit(solution)/shard_map/ppermute | solution.py:23
  21.9 3.3 %collective-permute-start.6 = (bf16[128,1792]{1,0:T(8,128)(2,1)S(1)}, bf16[128,1792]{1,0:T(8,128)(2,1)}, u32[]{:S(2)}, u32[]{:S(2)}) collective-permute-start(bf16[128,1792]{1,0:T(8,128)(2,1)S(1)} %constant_dynamic-slice_fusion.2.rest_0_), channel_id=1, source_target_pairs={{0,1},{1,2},{2,3},{3,0},{4,5},{5,6},{6,7},{7,4},{8,9},{9,10},{10,1... | collective-permute-start | bytes 1376264 | tf_op jit(solution)/shard_map/ppermute | solution.py:553
  32.7 8.6 %all-to-all-start = ((bf16[8,2,8,512]{3,2,1,0:T(8,128)(2,1)}), bf16[8,2,8,512]{3,2,1,0:T(8,128)(2,1)S(1)}, u32[]{:S(2)}, u32[]{:S(2)}) async-start(bf16[8,2,8,512]{3,2,1,0:T(8,128)(2,1)} %shard_map.210), calls=%async_computation | async-start | bytes 262144 | tf_op jit(solution)/shard_map/all_to_all | solution.py:27
  45.8 4.5 %all-to-all-done = bf16[8,2,8,512]{3,2,1,0:T(8,128)(2,1)S(1)} async-done(((bf16[8,2,8,512]{3,2,1,0:T(8,128)(2,1)}), bf16[8,2,8,512]{3,2,1,0:T(8,128)(2,1)S(1)}, u32[]{:S(2)}, u32[]{:S(2)}) %all-to-all-start) | async-done | bytes 131104 | tf_op jit(solution)/shard_map/all_to_all | solution.py:27
  52.7 8.4 %all_to_all.35 = bf16[4,32,512]{2,1,0:T(8,128)(2,1)S(1)} all-to-all(bf16[4,32,512]{2,1,0:T(8,128)(2,1)S(1)} %shard_map.214), channel_id=1, replica_groups=mesh['pd'=2,'dp'=4,'ep'=32] {'dp'}, dimensions={0} | all-to-all | bytes 262144 | tf_op jit(solution)/shard_map/all_to_all | solution.py:27
  65.5 4.1 %all-to-all-start.2 = ((bf16[8,8,1792]{2,1,0:T(8,128)(2,1)}), bf16[8,8,1792]{2,1,0:T(8,128)(2,1)S(1)}, u32[]{:S(2)}, u32[]{:S(2)}) async-start(bf16[8,8,1792]{2,1,0:T(8,128)(2,1)} %fusion), calls=%async_computation.2 | async-start | bytes 458752 | tf_op jit(solution)/shard_map/all_to_all | solution.py:27
  70.4 10.7 %all-to-all-done.2.sums_ref = bf16[8,8,1792]{2,1,0:T(8,128)(2,1)S(1)} async-done(((bf16[8,8,1792]{2,1,0:T(8,128)(2,1)}), bf16[8,8,1792]{2,1,0:T(8,128)(2,1)S(1)}, u32[]{:S(2)}, u32[]{:S(2)}) %all-to-all-start.2) | async-done | bytes 229408 | tf_op jit(solution)/shard_map/all_to_all | solution.py:27
  82.8 3.4 %all-to-all-start.3 = ((bf16[8,8,1920]{2,1,0:T(8,128)(2,1)}), bf16[8,8,1920]{2,1,0:T(8,128)(2,1)S(1)}, u32[]{:S(2)}, u32[]{:S(2)}) async-start(bf16[8,8,1920]{2,1,0:T(8,128)(2,1)} %get-tuple-element.136), calls=%async_computation.3 | async-start | bytes 491520 | tf_op jit(solution)/shard_map/all_to_all | solution.py:27
  86.2 2.2 %collective-permute-start.18 = (bf16[128,1792]{1,0:T(8,128)(2,1)}, bf16[128,1792]{1,0:T(8,128)(2,1)S(1)}, u32[]{:S(2)}, u32[]{:S(2)}) collective-permute-start(bf16[128,1792]{1,0:T(8,128)(2,1)} %get-tuple-element.141), channel_id=1, source_target_pairs={{0,64},{32,96},{64,0},{96,32},{1,65},{33,97},{65,1},{97,33},{2,66}... | collective-permute-start | bytes 1376264 | tf_op jit(solution)/shard_map/ppermute | solution.py:23
  89.6 7.1 %all-to-all-done.3 = bf16[8,8,1920]{2,1,0:T(8,128)(2,1)S(1)} async-done(((bf16[8,8,1920]{2,1,0:T(8,128)(2,1)}), bf16[8,8,1920]{2,1,0:T(8,128)(2,1)S(1)}, u32[]{:S(2)}, u32[]{:S(2)}) %all-to-all-start.3) | async-done | bytes 245792 | tf_op jit(solution)/shard_map/all_to_all | solution.py:27
  98.6 2.9 %collective-permute-start.15 = (bf16[64,1920]{1,0:T(8,128)(2,1)S(1)}, bf16[64,1920]{1,0:T(8,128)(2,1)S(1)}, u32[]{:S(2)}, u32[]{:S(2)}) collective-permute-start(bf16[64,1920]{1,0:T(8,128)(2,1)S(1)} %bitcast.45), channel_id=1, source_target_pairs={{0,2},{1,3},{2,0},{3,1},{4,6},{5,7},{6,4},{7,5},{8,10},{9,11},{10,... | collective-permute-start | bytes 737288 | tf_op jit(solution)/shard_map/ppermute | solution.py:553
  101.5 5.9 %collective-permute-done.18.rest_2_ = bf16[128,1792]{1,0:T(8,128)(2,1)S(1)} collective-permute-done((bf16[128,1792]{1,0:T(8,128)(2,1)}, bf16[128,1792]{1,0:T(8,128)(2,1)S(1)}, u32[]{:S(2)}, u32[]{:S(2)}) %collective-permute-start.18) | collective-permute-done | bytes 458784 | tf_op jit(solution)/shard_map/ppermute | solution.py:23
  109.0 3.3 %collective-permute-done.16.rest_3_ = bf16[64,1920]{1,0:T(8,128)(2,1)S(1)} collective-permute-done((bf16[64,1920]{1,0:T(8,128)(2,1)S(1)}, bf16[64,1920]{1,0:T(8,128)(2,1)S(1)}, u32[]{:S(2)}, u32[]{:S(2)}) %collective-permute-start.16) | collective-permute-done | bytes 245792 | tf_op jit(solution)/shard_map/ppermute | solution.py:553
  116.8 2.7 %shard_map.218 = bf16[4,64,1152]{2,1,0:T(8,128)(2,1)S(1)} custom-call(s32[1]{0:T(128)} %bitcast.at_ref, bf16[128,1920]{1,0:T(8,128)(2,1)S(1)} %shard_map.217.own_ref, bf16[128,1920]{1,0:T(8,128)(2,1)S(1)} %collective-permute-done.20.other_ref, bf16[1792,256]{1,0:T(8,128)(2,1)S(1)} %copy-done.2, bf16[1792,256]{1,0:T(8,128)(2,1)} %collective-permute-done.10.rest_1_, ...), custom_call_target="tpu_custom_call" | custom-call | tf_op jit(solution)/shard_map/pallas_call | solution.py:431
  119.5 13.3 %all_to_all.36.sums_ref = bf16[4,64,1152]{2,1,0:T(8,128)(2,1)S(1)} all-to-all(bf16[4,64,1152]{2,1,0:T(8,128)(2,1)S(1)} %shard_map.218), channel_id=1, replica_groups=mesh['pd'=2,'dp'=4,'ep'=32] {'dp'}, dimensions={0} | all-to-all | bytes 1179648 | tf_op jit(solution)/shard_map/all_to_all | solution.py:27
  133.0 9.1 %all_to_all.37.acts_ref = bf16[4,64,512]{2,1,0:T(8,128)(2,1)S(1)} all-to-all(bf16[4,64,512]{2,1,0:T(8,128)(2,1)S(1)} %shard_map.219), channel_id=1, replica_groups=mesh['pd'=2,'dp'=4,'ep'=32] {'dp'}, dimensions={0} | all-to-all | bytes 524288 | tf_op jit(solution)/shard_map/all_to_all | solution.py:27
  142.1 3.1 %shard_map.220 = (f32[128,1792]{1,0:T(8,128)S(1)}, bf16[128,1792]{1,0:T(8,128)(2,1)}) custom-call(s32[1]{0:T(128)} %bitcast.at_ref, bf16[4,64,512]{2,1,0:T(8,128)(2,1)S(1)} %all_to_all.37.acts_ref, bf16[128,1792]{1,0:T(8,128)(2,1)S(1)} %copy-done.4, bf16[128,1792]{1,0:T(8,128)(2,1)} %collective-permute-done.17.rest_1_, ...), custom_call_target="tpu_custom_call" | custom-call | tf_op jit(solution)/shard_map/pallas_call | solution.py:466
  149.3 3.0 %collective-permute-start.23 = (bf16[64,1792]{1,0:T(8,128)(2,1)S(1)}, bf16[64,1792]{1,0:T(8,128)(2,1)S(1)}, u32[]{:S(2)}, u32[]{:S(2)}) collective-permute-start(bf16[64,1792]{1,0:T(8,128)(2,1)S(1)} %get-tuple-element.160), channel_id=1, source_target_pairs={{0,2},{1,3},{2,0},{3,1},{4,6},{5,7},{6,4},{7,5},{8,10},{9,11},{10,... | collective-permute-start | bytes 688136 | tf_op jit(solution)/shard_map/ppermute | solution.py:553
  152.3 4.9 %collective-permute-done.22.rest_1_ = bf16[64,1792]{1,0:T(8,128)(2,1)S(1)} collective-permute-done((bf16[64,1792]{1,0:T(8,128)(2,1)S(1)}, bf16[64,1792]{1,0:T(8,128)(2,1)S(1)}, u32[]{:S(2)}, u32[]{:S(2)}) %collective-permute-start.22) | collective-permute-done | bytes 229408 | tf_op jit(solution)/shard_map/ppermute | solution.py:553
  159.3 3.8 %collective-permute-done.24.rest_3_ = bf16[64,1792]{1,0:T(8,128)(2,1)S(1)} collective-permute-done((bf16[64,1792]{1,0:T(8,128)(2,1)S(1)}, bf16[64,1792]{1,0:T(8,128)(2,1)S(1)}, u32[]{:S(2)}, u32[]{:S(2)}) %collective-permute-start.24) | collective-permute-done | bytes 229408 | tf_op jit(solution)/shard_map/ppermute | solution.py:553
  163.7 16.8 %all_to_all.38 = bf16[32,2,1792]{2,1,0:T(2,128)(2,1)S(1)} all-to-all(bf16[32,2,1792]{2,1,0:T(2,128)(2,1)S(1)} %reshape.32), channel_id=1, replica_groups={{0,4,8,12,16,20,24,28,32,36,40,44,48,52,56,60,64,68,72,76,80,84,88,92,9..., dimensions={0} | all-to-all | bytes 458752 | tf_op jit(solution)/shard_map/all_to_all | solution.py:27
  (108 shorter events, 43.4 us)
Async XLA Ops:
  2.5 7.1 %collective-permute-start = (bf16[80,640]{1,0:T(8,128)(2,1)S(1)}, bf16[80,640]{1,0:T(8,128)(2,1)S(1)}, u32[]{:S(2)}, u32[]{:S(2)}) collective-permute-start(bf16[80,640]{1,0:T(8,128)(2,1)S(1)} %get-tuple-element.82), channel_id=1, source_target_pairs={{0,32},{32,64},{64,96},{96,0},{1,33},{33,65},{65,97},{97,1},{2,34}... | collective-permute-start | bytes 307208 | tf_op jit(solution)/shard_map/ppermute | solution.py:23
  4.1 14.4 %collective-permute-start.3 = (bf16[512,128]{1,0:T(8,128)(2,1)}, bf16[512,128]{1,0:T(8,128)(2,1)}, u32[]{:S(2)}, u32[]{:S(2)}) collective-permute-start(bf16[512,128]{1,0:T(8,128)(2,1)} %bitcast.55), channel_id=1, source_target_pairs={{0,1},{1,2},{2,3},{3,0},{4,5},{5,6},{6,7},{7,4},{8,9},{9,10},{10,1... | collective-permute-start | bytes 393224 | tf_op jit(solution)/shard_map/ppermute | solution.py:553
  4.6 13.8 %collective-permute-start.4 = (bf16[512,128]{1,0:T(8,128)(2,1)}, bf16[512,128]{1,0:T(8,128)(2,1)}, u32[]{:S(2)}, u32[]{:S(2)}) collective-permute-start(bf16[512,128]{1,0:T(8,128)(2,1)} %bitcast.56), channel_id=1, source_target_pairs={{0,2},{1,3},{2,0},{3,1},{4,6},{5,7},{6,4},{7,5},{8,10},{9,11},{10,... | collective-permute-start | bytes 393224 | tf_op jit(solution)/shard_map/ppermute | solution.py:553
  6.9 11.6 %collective-permute-start.5 = (bf16[512,128]{1,0:T(8,128)(2,1)}, bf16[512,128]{1,0:T(8,128)(2,1)}, u32[]{:S(2)}, u32[]{:S(2)}) collective-permute-start(bf16[512,128]{1,0:T(8,128)(2,1)} %bitcast.57), channel_id=1, source_target_pairs={{0,3},{1,0},{2,1},{3,2},{4,7},{5,4},{6,5},{7,6},{8,11},{9,8},{10,9... | collective-permute-start | bytes 393224 | tf_op jit(solution)/shard_map/ppermute | solution.py:553
  6.9 11.5 %collective-permute-start.1 = (bf16[80,640]{1,0:T(8,128)(2,1)S(1)}, bf16[80,640]{1,0:T(8,128)(2,1)S(1)}, u32[]{:S(2)}, u32[]{:S(2)}) collective-permute-start(bf16[80,640]{1,0:T(8,128)(2,1)S(1)} %get-tuple-element.85), channel_id=1, source_target_pairs={{0,64},{32,96},{64,0},{96,32},{1,65},{33,97},{65,1},{97,33},{2,66}... | collective-permute-start | bytes 307208 | tf_op jit(solution)/shard_map/ppermute | solution.py:23
  9.6 8.8 %collective-permute-start.2 = (bf16[80,640]{1,0:T(8,128)(2,1)S(1)}, bf16[80,640]{1,0:T(8,128)(2,1)S(1)}, u32[]{:S(2)}, u32[]{:S(2)}) collective-permute-start(bf16[80,640]{1,0:T(8,128)(2,1)S(1)} %get-tuple-element.86), channel_id=1, source_target_pairs={{0,96},{32,0},{64,32},{96,64},{1,97},{33,1},{65,33},{97,65},{2,98}... | collective-permute-start | bytes 307208 | tf_op jit(solution)/shard_map/ppermute | solution.py:23
  18.5 42.6 %collective-permute-start.10 = (bf16[1792,256]{1,0:T(8,128)(2,1)}, bf16[1792,256]{1,0:T(8,128)(2,1)}, u32[]{:S(2)}, u32[]{:S(2)}) collective-permute-start(bf16[1792,256]{1,0:T(8,128)(2,1)} %get-tuple-element.125), channel_id=1, source_target_pairs={{0,32},{32,64},{64,96},{96,0},{1,33},{33,65},{65,97},{97,1},{2,34}... | collective-permute-start | bytes 2752520 | tf_op jit(solution)/shard_map/ppermute | solution.py:23
  19.1 41.9 %collective-permute-start.11 = (bf16[1792,256]{1,0:T(8,128)(2,1)}, bf16[1792,256]{1,0:T(8,128)(2,1)}, u32[]{:S(2)}, u32[]{:S(2)}) collective-permute-start(bf16[1792,256]{1,0:T(8,128)(2,1)} %get-tuple-element.126), channel_id=1, source_target_pairs={{0,96},{32,0},{64,32},{96,64},{1,97},{33,1},{65,33},{97,65},{2,98}... | collective-permute-start | bytes 2752520 | tf_op jit(solution)/shard_map/ppermute | solution.py:23
  21.9 28.5 %collective-permute-start.6 = (bf16[128,1792]{1,0:T(8,128)(2,1)S(1)}, bf16[128,1792]{1,0:T(8,128)(2,1)}, u32[]{:S(2)}, u32[]{:S(2)}) collective-permute-start(bf16[128,1792]{1,0:T(8,128)(2,1)S(1)} %constant_dynamic-slice_fusion.2.rest_0_), channel_id=1, source_target_pairs={{0,1},{1,2},{2,3},{3,0},{4,5},{5,6},{6,7},{7,4},{8,9},{9,10},{10,1... | collective-permute-start | bytes 1376264 | tf_op jit(solution)/shard_map/ppermute | solution.py:553
  25.2 25.2 %collective-permute-start.7 = (bf16[128,1792]{1,0:T(8,128)(2,1)S(1)}, bf16[128,1792]{1,0:T(8,128)(2,1)}, u32[]{:S(2)}, u32[]{:S(2)}) collective-permute-start(bf16[128,1792]{1,0:T(8,128)(2,1)S(1)} %constant_dynamic-slice_fusion.2.rest_0_), channel_id=1, source_target_pairs={{0,3},{1,0},{2,1},{3,2},{4,7},{5,4},{6,5},{7,6},{8,11},{9,8},{10,9... | collective-permute-start | bytes 1376264 | tf_op jit(solution)/shard_map/ppermute | solution.py:553
  25.2 27.5 %collective-permute-start.9 = (bf16[128,1792]{1,0:T(8,128)(2,1)S(1)}, bf16[128,1792]{1,0:T(8,128)(2,1)}, u32[]{:S(2)}, u32[]{:S(2)}) collective-permute-start(bf16[128,1792]{1,0:T(8,128)(2,1)S(1)} %constant_dynamic-slice_fusion.2.rest_0_), channel_id=1, source_target_pairs={{0,2},{1,3},{2,0},{3,1},{4,6},{5,7},{6,4},{7,5},{8,10},{9,11},{10,... | collective-permute-start | bytes 1376264 | tf_op jit(solution)/shard_map/ppermute | solution.py:553
  32.7 17.7 %all-to-all-start = ((bf16[8,2,8,512]{3,2,1,0:T(8,128)(2,1)}), bf16[8,2,8,512]{3,2,1,0:T(8,128)(2,1)S(1)}, u32[]{:S(2)}, u32[]{:S(2)}) async-start(bf16[8,2,8,512]{3,2,1,0:T(8,128)(2,1)} %shard_map.210), calls=%async_computation | async-start | bytes 262144 | tf_op jit(solution)/shard_map/all_to_all | solution.py:27
  63.3 26.3 %collective-permute-start.13 = (bf16[1792,256]{1,0:T(8,128)(2,1)}, bf16[1792,256]{1,0:T(8,128)(2,1)}, u32[]{:S(2)}, u32[]{:S(2)}) collective-permute-start(bf16[1792,256]{1,0:T(8,128)(2,1)} %get-tuple-element.137), channel_id=1, source_target_pairs={{0,64},{32,96},{64,0},{96,32},{1,65},{33,97},{65,1},{97,33},{2,66}... | collective-permute-start | bytes 2752520 | tf_op jit(solution)/shard_map/ppermute | solution.py:23
  65.5 15.6 %all-to-all-start.2 = ((bf16[8,8,1792]{2,1,0:T(8,128)(2,1)}), bf16[8,8,1792]{2,1,0:T(8,128)(2,1)S(1)}, u32[]{:S(2)}, u32[]{:S(2)}) async-start(bf16[8,8,1792]{2,1,0:T(8,128)(2,1)} %fusion), calls=%async_computation.2 | async-start | bytes 458752 | tf_op jit(solution)/shard_map/all_to_all | solution.py:27
  69.6 31.9 %collective-permute-start.17 = (bf16[128,1792]{1,0:T(8,128)(2,1)}, bf16[128,1792]{1,0:T(8,128)(2,1)}, u32[]{:S(2)}, u32[]{:S(2)}) collective-permute-start(bf16[128,1792]{1,0:T(8,128)(2,1)} %get-tuple-element.140), channel_id=1, source_target_pairs={{0,32},{32,64},{64,96},{96,0},{1,33},{33,65},{65,97},{97,1},{2,34}... | collective-permute-start | bytes 1376264 | tf_op jit(solution)/shard_map/ppermute | solution.py:23
  82.8 13.9 %all-to-all-start.3 = ((bf16[8,8,1920]{2,1,0:T(8,128)(2,1)}), bf16[8,8,1920]{2,1,0:T(8,128)(2,1)S(1)}, u32[]{:S(2)}, u32[]{:S(2)}) async-start(bf16[8,8,1920]{2,1,0:T(8,128)(2,1)} %get-tuple-element.136), calls=%async_computation.3 | async-start | bytes 491520 | tf_op jit(solution)/shard_map/all_to_all | solution.py:27
  86.2 21.3 %collective-permute-start.18 = (bf16[128,1792]{1,0:T(8,128)(2,1)}, bf16[128,1792]{1,0:T(8,128)(2,1)S(1)}, u32[]{:S(2)}, u32[]{:S(2)}) collective-permute-start(bf16[128,1792]{1,0:T(8,128)(2,1)} %get-tuple-element.141), channel_id=1, source_target_pairs={{0,64},{32,96},{64,0},{96,32},{1,65},{33,97},{65,1},{97,33},{2,66}... | collective-permute-start | bytes 1376264 | tf_op jit(solution)/shard_map/ppermute | solution.py:23
  88.4 19.4 %collective-permute-start.19 = (bf16[128,1792]{1,0:T(8,128)(2,1)}, bf16[128,1792]{1,0:T(8,128)(2,1)}, u32[]{:S(2)}, u32[]{:S(2)}) collective-permute-start(bf16[128,1792]{1,0:T(8,128)(2,1)} %get-tuple-element.142), channel_id=1, source_target_pairs={{0,96},{32,0},{64,32},{96,64},{1,97},{33,1},{65,33},{97,65},{2,98}... | collective-permute-start | bytes 1376264 | tf_op jit(solution)/shard_map/ppermute | solution.py:23
  96.7 11.1 %collective-permute-start.14 = (bf16[64,1920]{1,0:T(8,128)(2,1)S(1)}, bf16[64,1920]{1,0:T(8,128)(2,1)S(1)}, u32[]{:S(2)}, u32[]{:S(2)}) collective-permute-start(bf16[64,1920]{1,0:T(8,128)(2,1)S(1)} %bitcast.44), channel_id=1, source_target_pairs={{0,1},{1,2},{2,3},{3,0},{4,5},{5,6},{6,7},{7,4},{8,9},{9,10},{10,1... | collective-permute-start | bytes 737288 | tf_op jit(solution)/shard_map/ppermute | solution.py:553
  98.6 10.4 %collective-permute-start.15 = (bf16[64,1920]{1,0:T(8,128)(2,1)S(1)}, bf16[64,1920]{1,0:T(8,128)(2,1)S(1)}, u32[]{:S(2)}, u32[]{:S(2)}) collective-permute-start(bf16[64,1920]{1,0:T(8,128)(2,1)S(1)} %bitcast.45), channel_id=1, source_target_pairs={{0,2},{1,3},{2,0},{3,1},{4,6},{5,7},{6,4},{7,5},{8,10},{9,11},{10,... | collective-permute-start | bytes 737288 | tf_op jit(solution)/shard_map/ppermute | solution.py:553
  101.5 10.8 %collective-permute-start.16 = (bf16[64,1920]{1,0:T(8,128)(2,1)S(1)}, bf16[64,1920]{1,0:T(8,128)(2,1)S(1)}, u32[]{:S(2)}, u32[]{:S(2)}) collective-permute-start(bf16[64,1920]{1,0:T(8,128)(2,1)S(1)} %bitcast.46), channel_id=1, source_target_pairs={{0,3},{1,0},{2,1},{3,2},{4,7},{5,4},{6,5},{7,6},{8,11},{9,8},{10,9... | collective-permute-start | bytes 737288 | tf_op jit(solution)/shard_map/ppermute | solution.py:553
  148.7 8.5 %collective-permute-start.22 = (bf16[64,1792]{1,0:T(8,128)(2,1)S(1)}, bf16[64,1792]{1,0:T(8,128)(2,1)S(1)}, u32[]{:S(2)}, u32[]{:S(2)}) collective-permute-start(bf16[64,1792]{1,0:T(8,128)(2,1)S(1)} %get-tuple-element.161), channel_id=1, source_target_pairs={{0,1},{1,2},{2,3},{3,0},{4,5},{5,6},{6,7},{7,4},{8,9},{9,10},{10,1... | collective-permute-start | bytes 688136 | tf_op jit(solution)/shard_map/ppermute | solution.py:553
  149.3 10.0 %collective-permute-start.23 = (bf16[64,1792]{1,0:T(8,128)(2,1)S(1)}, bf16[64,1792]{1,0:T(8,128)(2,1)S(1)}, u32[]{:S(2)}, u32[]{:S(2)}) collective-permute-start(bf16[64,1792]{1,0:T(8,128)(2,1)S(1)} %get-tuple-element.160), channel_id=1, source_target_pairs={{0,2},{1,3},{2,0},{3,1},{4,6},{5,7},{6,4},{7,5},{8,10},{9,11},{10,... | collective-permute-start | bytes 688136 | tf_op jit(solution)/shard_map/ppermute | solution.py:553
  152.3 10.8 %collective-permute-start.24 = (bf16[64,1792]{1,0:T(8,128)(2,1)S(1)}, bf16[64,1792]{1,0:T(8,128)(2,1)S(1)}, u32[]{:S(2)}, u32[]{:S(2)}) collective-permute-start(bf16[64,1792]{1,0:T(8,128)(2,1)S(1)} %get-tuple-element.159), channel_id=1, source_target_pairs={{0,3},{1,0},{2,1},{3,2},{4,7},{5,4},{6,5},{7,6},{8,11},{9,8},{10,9... | collective-permute-start | bytes 688136 | tf_op jit(solution)/shard_map/ppermute | solution.py:553
  (27 other events, 291.9 us)
where the time goes:
time: 182 us; the launch traced here: 181 us
  waiting for transfers between devices  49.4 us (27%)
  starting transfers between devices  47.5 us (26%)
  blocking collectives  47.5 us (26%)
  Pallas kernels  21.7 us (12%)
  local copies, waits for them, and re-layouts  9.89 us (5%)
  other arithmetic  2.8 us (2%)
  between operations  2.5 us (1%)
    all_to_all x4, blocking collectives, exchange(): return lax.all_to_all(value, axis, 0, 0, axis_index_groups=groups)  47.5 us
    all_to_all x3, waiting for transfers between devices, exchange(): return lax.all_to_all(value, axis, 0, 0, axis_index_groups=groups)  22.3 us
    ppermute x12, starting transfers between devices, shift_y(): return lax.ppermute(value, 'ep', pairs)  16.7 us
    all_to_all x3, starting transfers between devices, exchange(): return lax.all_to_all(value, axis, 0, 0, axis_index_groups=groups)  16.1 us
    ppermute x12, waiting for transfers between devices, shift_y(): return lax.ppermute(value, 'ep', pairs)  15.4 us
    ppermute x13, starting transfers between devices, shift(): lax.ppermute(value, axis, [(i, (i + amount) % size) for i in range(size)])  14.7 us
    ppermute x13, waiting for transfers between devices, shift(): lax.ppermute(value, axis, [(i, (i + amount) % size) for i in range(size)])  11.7 us
    unnamed x46, local copies, waits for them, and re-layouts  8.9 us
  transfers between devices with their start and end apart: 28, of which 14 were waited for; matrix products, arithmetic and copies ran while one was open for 2% of the time, Pallas kernels for 6%

commit v1 on v0

--- a/solution.py
+++ b/solution.py
@@ -138,14 +138,16 @@
 def old_kernel(lines, at_ref, len_ref, query_ref, order_ref, keys_ref, scales_ref, *rest):
     gate_ref, up_ref, down_ref, out_ref = rest[:4]
     outs, held_ref, sems = rest[4:-2], rest[-2], rest[-1]
-    cols, units = outs[1].shape[1], gate_ref.shape[1]
+    cols, units = gate_ref.shape[0] // lines, gate_ref.shape[1]
     copies = []
-    for s in range(lines):
+    for s, out in enumerate(outs):
         start = pl.multiple_of(lax.rem(at_ref[0] + s, lines) * cols, 128)
-        both, down = outs[2 * s], outs[2 * s + 1]
-        copies.append((gate_ref.at[pl.ds(start, cols)], both.at[:, pl.ds(0, units)]))
-        copies.append((up_ref.at[pl.ds(start, cols)], both.at[:, pl.ds(units, units)]))
-        copies.append((down_ref.at[:, pl.ds(start, cols)], down))
+        copies.append((gate_ref.at[pl.ds(start, cols)], out.at[pl.ds(0, cols), pl.ds(0, units)]))
+        copies.append((up_ref.at[pl.ds(start, cols)], out.at[pl.ds(0, cols), pl.ds(units, units)]))
+        for block in range(cols // 256):
+            at = pl.multiple_of(start + block * 256, 128)
+            to = out.at[pl.ds(cols + block * units, units)]
+            copies.append((down_ref.at[:, pl.ds(at, 256)], to))
     copies = [pltpu.make_async_copy(a, b, sems.at[i]) for i, (a, b) in enumerate(copies)]
     for copy in copies:
         copy.start()
@@ -164,12 +166,12 @@
     return pl.pallas_call(
         functools.partial(old_kernel, lines),
         out_shape=[shape((pieces, rows, DLAT), BF16)]
-        + [shape((cols, 2 * units), BF16), shape((units, cols), BF16)] * lines,
+        + [shape((cols + cols // 256 * units, 256), BF16)] * lines,
         in_specs=[SMEM, SMEM] + [VMEM] * 4 + [HBM] * 3,
-        out_specs=[VMEM] * (2 * lines + 1),
+        out_specs=[VMEM] * (lines + 1),
         scratch_shapes=[
             pltpu.VMEM((DLAT, keys.shape[1]), BF16),
-            pltpu.SemaphoreType.DMA((3 * lines,)),
+            pltpu.SemaphoreType.DMA(((2 + cols // 256) * lines,)),
         ],
         compiler_params=WIDE,
         cost_estimate=pl.CostEstimate(
@@ -201,7 +203,7 @@
         in_specs=[SMEM, SMEM] + [VMEM] * (4 + len(parcels)),
         out_specs=VMEM,
         scratch_shapes=[pltpu.VMEM((DLAT, keys.shape[1]), BF16)],
-        compiler_params=PARAMS,
+        compiler_params=WIDE,
     )(step, length, order, keys, scales, old, *parcels)
 
 
@@ -405,7 +407,10 @@
 def gate_up_kernel(lines, at_ref, own_ref, other_ref, *rest):
     parts, out_ref, held, sems = rest[:-3], rest[-3], rest[-2], rest[-1]
     cols, lanes = held.shape[1:]
-    copies = [pltpu.make_async_copy(parts[s], held.at[s], sems.at[s]) for s in range(lines)]
+    copies = [
+        pltpu.make_async_copy(parts[s].at[pl.ds(0, cols)], held.at[s], sems.at[s])
+        for s in range(lines)
+    ]
     for copy in copies:
         copy.start()
     for s in range(lines):
@@ -427,7 +432,7 @@
 
 
 def gate_up(dp, own, other, parts):
-    lines, (cols, lanes) = len(parts), parts[0].shape
+    lines, cols, lanes = len(parts), own.shape[1] - 128, parts[0].shape[1]
     return pl.pallas_call(
         functools.partial(gate_up_kernel, lines),
         out_shape=shape((lines, 2 * own.shape[0] // lines, lines * lanes + 128), BF16),
@@ -443,11 +448,15 @@
 
 def down_kernel(lines, at_ref, acts_ref, *rest):
     parts, own_ref, other_ref, held, sems = rest[:-4], rest[-4], rest[-3], rest[-2], rest[-1]
-    units, cols = parts[0].shape
+    blocks, units = held.shape[0], held.shape[1] // lines
     copies = []
     for s in range(lines):
         row = pl.multiple_of(lax.rem(at_ref[0] - s + lines, lines) * units, 128)
-        copies.append(pltpu.make_async_copy(parts[s], held.at[pl.ds(row, units)], sems.at[s]))
+        for block in range(blocks):
+            at = blocks * 256 + block * units
+            part = parts[s].at[pl.ds(at, units)]
+            to = held.at[block, pl.ds(row, units)]
+            copies.append(pltpu.make_async_copy(part, to, sems.at[s * blocks + block]))
     for copy in copies:
         copy.start()
     for copy in copies:
@@ -455,22 +464,23 @@
     capacity = acts_ref.shape[1] // 2
     own = jnp.concatenate([acts_ref[d, :capacity] for d in range(lines)], axis=0)
     other = jnp.concatenate([acts_ref[d, capacity:] for d in range(lines)], axis=0)
-    for at in range(0, cols, 256):
-        own_ref[:, at : at + 256] = dot(own, held[:, at : at + 256])
-        other_ref[:, at : at + 256] = dot(other, held[:, at : at + 256]).astype(BF16)
-
-
-def down(dp, acts, parts):
-    lines, (units, cols) = len(parts), parts[0].shape
+    for block in range(blocks):
+        at = block * 256
+        own_ref[:, at : at + 256] = dot(own, held[block]).astype(BF16)
+        other_ref[:, at : at + 256] = dot(other, held[block]).astype(BF16)
+
+
+def down(dp, acts, parts, cols):
+    lines, units = len(parts), acts.shape[2] // len(parts)
     slots = acts.shape[0] * acts.shape[1] // 2
     return pl.pallas_call(
         functools.partial(down_kernel, lines),
-        out_shape=[shape((slots, cols), F32), shape((slots, cols), BF16)],
+        out_shape=[shape((slots, cols), BF16), shape((slots, cols), BF16)],
         in_specs=[SMEM, VMEM] + [ANY] * lines,
         out_specs=[VMEM, VMEM],
         scratch_shapes=[
-            pltpu.VMEM((lines * units, cols), BF16),
-            pltpu.SemaphoreType.DMA((lines,)),
+            pltpu.VMEM((cols // 256, lines * units, 256), BF16),
+            pltpu.SemaphoreType.DMA((lines * (cols // 256),)),
         ],
         compiler_params=PARAMS,
     )(dp, acts, *parts)
@@ -478,7 +488,7 @@
 
 def expand_kernel(own_ref, other_ref, gate_ref, select_ref, out_ref):
     for at in range(0, own_ref.shape[1], 256):
-        total = own_ref[:, at : at + 256] + other_ref[:, at : at + 256].astype(F32)
+        total = own_ref[:, at : at + 256].astype(F32) + other_ref[:, at : at + 256].astype(F32)
         weighted = (total * gate_ref[...]).astype(BF16)
         out_ref[:, at : at + 256] = dot(select_ref[...], weighted).astype(BF16)
 
@@ -555,7 +565,6 @@
     at_dp = dp.astype(jnp.int32).reshape(1)
     parcels = make_parcels(at_dp, n_dp, fresh_owner, queries, hidden)
     parcels = list(parcels[:1]) + [shift(parcels[s], "dp", s) for s in range(1, n_dp)]
-    gain = lax.dynamic_slice_in_dim(norm_gain, dp * cols, cols, 0)[None]
 
     whole, first = lax.optimization_barrier((queries, parcels[1]))
 
@@ -582,17 +591,17 @@
     old_out, rest, uv_parts = lax.optimization_barrier((old_out, parcels[2:], uv_parts))
     parcels = [parcels[0], first] + list(rest)
     parcels, packed = lax.optimization_barrier((parcels, packed))
-    both_parts = [packed[0]] + [shift(packed[2 * s], "dp", s) for s in range(1, n_dp)]
-    down_parts = [packed[1]] + [shift(packed[2 * s + 1], "dp", s) for s in range(1, n_dp)]
+    parts = [packed[0]] + [shift(packed[s], "dp", s) for s in range(1, n_dp)]
     step = (dp - fresh_owner) % n_dp
     latent = new_attention(
         step, fresh_len, order, fresh_vals[0].T, fresh_scales[0], old_out, parcels
     )
     slab = 2 * n_ep
     capacity = 2 * slab * route_ids.shape[1] // n_ep
-    latent, ids, gates, parcels = lax.optimization_barrier(
-        (latent, route_ids.T, route_weights.T, parcels)
-    )
+    latent, ids, gates, parcels, norm_gain = lax.optimization_barrier(
+        (latent, route_ids.T, route_weights.T, parcels, norm_gain)
+    )
+    gain = lax.dynamic_slice_in_dim(norm_gain, dp * cols, cols, 0)[None]
     at = jnp.stack([pd, ep, place_y, ep // chips_y]).astype(jnp.int32)
     masks = make_masks(
         at,
@@ -611,7 +620,7 @@
     values, far = lax.optimization_barrier((values, out_parts[2]))
     out_parts = [out_own, near[0], far, near[1]]
     values = exchange(values, "dp")
-    values, near = lax.optimization_barrier((values, both_parts[1::2]))
+    values, near = lax.optimization_barrier((values, parts[1::2]))
     rows = n_dp * 2 * chips_z * 2
     order = np.arange(rows).reshape(n_dp, 2, chips_z, 2).transpose(1, 2, 0, 3).reshape(rows)
     order = jnp.asarray(np.eye(rows)[order], BF16)
@@ -620,24 +629,23 @@
     summands = exchange(partial.reshape(chips_z, n_dp * 2, cols), "ep", z_groups)
     resid_cols, parcel = residual(summands, line)
     column = exchange(parcel, "ep", z_groups)
-    column, far = lax.optimization_barrier((column, both_parts[2]))
-    both_parts = [both_parts[0], near[0], far, near[1]]
+    column, far = lax.optimization_barrier((column, parts[2]))
+    parts = [parts[0], near[0], far, near[1]]
     column = column.reshape(chips_z * n_dp * 2, cols + 128)
     columns = [column] + [shift_y(column, s) for s in range(1, chips_y)]
-    columns, down_parts = lax.optimization_barrier((columns, down_parts))
     slot_rows = select_rows(at, select, columns)
     other_rows = shift(slot_rows, "pd", 1)
 
-    halves = gate_up(at_dp, slot_rows, other_rows, both_parts)
+    halves = gate_up(at_dp, slot_rows, other_rows, parts)
     all_acts = exchange(activations(width, units, exchange(halves, "dp")), "dp")
-    own, other = down(at_dp, all_acts, down_parts)
+    own, other = down(at_dp, all_acts, parts, cols)
     table = expand(own, shift(other, "pd", 1), slot_gate, select_back)
     table = table.reshape(chips_y, n_dp * chips_z * 2, cols)
-    parts = [lax.dynamic_index_in_dim(table, place_y, 0, keepdims=False)]
+    pieces = [lax.dynamic_index_in_dim(table, place_y, 0, keepdims=False)]
     for s in range(1, chips_y):
         part = lax.dynamic_index_in_dim(table, (place_y + s) % chips_y, 0, keepdims=False)
-        parts.append(shift_y(part, s))
-    table = join(own_line, resid_cols, parts).reshape(n_dp * chips_z, 2, cols)
+        pieces.append(shift_y(part, s))
+    table = join(own_line, resid_cols, pieces).reshape(n_dp * chips_z, 2, cols)
     planes = [
         [d * n_ep + z * chips_y + y for d in range(n_dp) for z in range(chips_z)]
         for y in range(chips_y)

time: 182 us -> 193 us (1.060)
  blocking collectives: 47.5 us -> 69.3 us
  waiting for transfers between devices: 49.4 us -> 36.4 us
  starting transfers between devices: 47.5 us -> 38 us
  local copies, waits for them, and re-layouts: 9.89 us -> 19.2 us
  Pallas kernels: 21.7 us -> 23.8 us
    all_to_all x4 -> x5, blocking collectives: 47.5 us -> 69.3 us  [exchange(): return lax.all_to_all(value, axis, 0, 0, axis_index_groups=groups)]
    all_to_all x3 -> x2, waiting for transfers between devices: 22.3 us -> 1.29 us  [exchange(): return lax.all_to_all(value, axis, 0, 0, axis_index_groups=groups)]
    unnamed x46 -> x68, local copies, waits for them, and re-layouts: 8.9 us -> 16 us
    ppermute x12, waiting for transfers between devices: 15.4 us -> 20.4 us  [shift_y(): return lax.ppermute(value, 'ep', pairs)]
    ppermute x13 -> x10, starting transfers between devices: 14.7 us -> 10.3 us  [shift(): lax.ppermute(value, axis, [(i, (i + amount) % size) for i in range(size)])]
    all_to_all x3 -> x2, starting transfers between devices: 16.1 us -> 11.9 us  [exchange(): return lax.all_to_all(value, axis, 0, 0, axis_index_groups=groups)]
    ppermute x13 -> x10, waiting for transfers between devices: 11.7 us -> 14.7 us  [shift(): lax.ppermute(value, axis, [(i, (i + amount) % size) for i in range(size)])]
  transfers between devices with their start and end apart: 28 -> 24, of which waited for: 14 -> 12; matrix products, arithmetic and copies ran while one was open for 2% -> 3% of each run, Pallas kernels for 6% -> 6%
where the time goes in v1:
time: 193 us; the launch traced here: 192 us
  blocking collectives  69.3 us (36%)
  starting transfers between devices  38 us (20%)
  waiting for transfers between devices  36.4 us (19%)
  Pallas kernels  23.8 us (12%)
  local copies, waits for them, and re-layouts  19.2 us (10%)
  other arithmetic  2.94 us (2%)
  between operations  2.46 us (1%)
    all_to_all x5, blocking collectives, exchange(): return lax.all_to_all(value, axis, 0, 0, axis_index_groups=groups)  69.3 us
    ppermute x12, waiting for transfers between devices, shift_y(): return lax.ppermute(value, 'ep', pairs)  20.4 us
    unnamed x68, local copies, waits for them, and re-layouts  16 us
    ppermute x12, starting transfers between devices, shift_y(): return lax.ppermute(value, 'ep', pairs)  15.8 us
    ppermute x10, waiting for transfers between devices, shift(): lax.ppermute(value, axis, [(i, (i + amount) % size) for i in range(size)])  14.7 us
    all_to_all x2, starting transfers between devices, exchange(): return lax.all_to_all(value, axis, 0, 0, axis_index_groups=groups)  11.9 us
    ppermute x10, starting transfers between devices, shift(): lax.ppermute(value, axis, [(i, (i + amount) % size) for i in range(size)])  10.3 us
    pallas_call x1, Pallas kernels, old_attention(): pl.pallas_call(functools.partial(old_kernel, lines), out_shape=[shape((pi...  6.74 us
  transfers between devices with their start and end apart: 24, of which 12 were waited for; matrix products, arithmetic and copies ran while one was open for 3% of the time, Pallas kernels for 6%

profile of v1, /device:TPU:24, one launch (start us, length us, event | category | flops | bytes accessed | tf_op | source)
XLA Modules:
  0.0 192.0 jit_solution(15879439537644124082)
XLA Ops:
  5.1 2.3 %collective-permute-start.4 = (bf16[512,128]{1,0:T(8,128)(2,1)}, bf16[512,128]{1,0:T(8,128)(2,1)S(1)}, u32[]{:S(2)}, u32[]{:S(2)}) collective-permute-start(bf16[512,128]{1,0:T(8,128)(2,1)} %bitcast.55), channel_id=1, source_target_pairs={{0,2},{1,3},{2,0},{3,1},{4,6},{5,7},{6,4},{7,5},{8,10},{9,11},{10,... | collective-permute-start | bytes 393224 | tf_op jit(solution)/shard_map/ppermute | solution.py:563
  7.5 2.7 %collective-permute-start.1 = (bf16[80,640]{1,0:T(8,128)(2,1)S(1)}, bf16[80,640]{1,0:T(8,128)(2,1)S(1)}, u32[]{:S(2)}, u32[]{:S(2)}) collective-permute-start(bf16[80,640]{1,0:T(8,128)(2,1)S(1)} %get-tuple-element.70), channel_id=1, source_target_pairs={{0,64},{32,96},{64,0},{96,32},{1,65},{33,97},{65,1},{97,33},{2,66}... | collective-permute-start | bytes 307208 | tf_op jit(solution)/shard_map/ppermute | solution.py:23
  12.3 6.7 %shard_map.209 = (bf16[8,8,512]{2,1,0:T(8,128)(2,1)}, bf16[2688,256]{1,0:T(8,128)(2,1)}, bf16[2688,256]{1,0:T(8,128)(2,1)}, bf16[2688,256]{1,0:T(8,128)(2,1)}, bf16[2688,256]{1,0:T(8,128)(2,1)}) custom-call(s32[1]{0:T(128)} %bitcast.at_ref, s32[1]{0:T(128)S(6)} %copy.23.len_ref, bf16[2,64,576]{2,1,0:T(8,128)(2,1)} %query_ref.2, ...), custom_call_target="tpu_custom_call" | custom-call | flops 150994944 | bytes 12189696 | tf_op jit(solution)/shard_map/pallas_call | solution.py:166
  20.4 2.6 %collective-permute-start.11 = (bf16[2688,256]{1,0:T(8,128)(2,1)}, bf16[2688,256]{1,0:T(8,128)(2,1)}, u32[]{:S(2)}, u32[]{:S(2)}) collective-permute-start(bf16[2688,256]{1,0:T(8,128)(2,1)} %get-tuple-element.108), channel_id=1, source_target_pairs={{0,96},{32,0},{64,32},{96,64},{1,97},{33,1},{65,33},{97,65},{2,98}... | collective-permute-start | bytes 4128776 | tf_op jit(solution)/shard_map/ppermute | solution.py:23
  23.9 3.2 %collective-permute-start.6 = (bf16[128,1792]{1,0:T(8,128)(2,1)}, bf16[128,1792]{1,0:T(8,128)(2,1)}, u32[]{:S(2)}, u32[]{:S(2)}) collective-permute-start(bf16[128,1792]{1,0:T(8,128)(2,1)} %constant_dynamic-slice_fusion.2.rest_0_), channel_id=1, source_target_pairs={{0,1},{1,2},{2,3},{3,0},{4,5},{5,6},{6,7},{7,4},{8,9},{9,10},{10,1... | collective-permute-start | bytes 1376264 | tf_op jit(solution)/shard_map/ppermute | solution.py:563
  30.1 3.1 %shard_map.210 = bf16[8,2,8,512]{3,2,1,0:T(8,128)(2,1)} custom-call(s32[1]{0:T(128)S(6)} %select_n.50.step_ref, s32[1]{0:T(128)S(6)} %copy.24.len_ref, bf16[64,64]{1,0:T(8,128)(2,1)} %constant.104.clone.order_ref, bf16[576,1024]{1,0:T(8,128)(2,1)} %bitcast.52, bf16[4,1024]{1,0:T(4,128)(2,1)} %bitcast.60, bf16[8,8,512]{2,1,0:T(8,128)(2,1)} %get-tuple-element.72.old_ref, ...), custom_call_target="tpu_custom_call" | custom-call | tf_op jit(solution)/shard_map/pallas_call | solution.py:200
  34.0 8.5 %all-to-all-start = ((bf16[8,2,8,512]{3,2,1,0:T(8,128)(2,1)}), bf16[8,2,8,512]{3,2,1,0:T(8,128)(2,1)S(1)}, u32[]{:S(2)}, u32[]{:S(2)}) async-start(bf16[8,2,8,512]{3,2,1,0:T(8,128)(2,1)} %shard_map.210), calls=%async_computation | async-start | bytes 262144 | tf_op jit(solution)/shard_map/all_to_all | solution.py:27
  59.2 8.4 %all_to_all.35 = bf16[4,32,512]{2,1,0:T(8,128)(2,1)S(1)} all-to-all(bf16[4,32,512]{2,1,0:T(8,128)(2,1)S(1)} %shard_map.214), channel_id=1, replica_groups=mesh['pd'=2,'dp'=4,'ep'=32] {'dp'}, dimensions={0} | all-to-all | bytes 262144 | tf_op jit(solution)/shard_map/all_to_all | solution.py:27
  67.5 2.7 %shard_map.215 = (f32[64,1792]{1,0:T(8,128)S(1)}, bf16[64,1792]{1,0:T(8,128)(2,1)S(1)}) custom-call(bf16[128,512]{1,0:T(8,128)(2,1)S(1)} %bitcast.48, bf16[128,128]{1,0:T(8,128)(2,1)S(1)} %copy-done.28, bf16[128,1792]{1,0:T(8,128)(2,1)} %constant_dynamic-slice_fusion.2.rest_0_, bf16[128,1792]{1,0:T(8,128)(2,1)} %collective-permute-done.6.rest_1_, ...), custom_call_target="tpu_custom_call" | custom-call | tf_op jit(solution)/shard_map/pallas_call | solution.py:274
  71.9 18.6 %all_to_all.36.sums_ref = bf16[8,8,1792]{2,1,0:T(8,128)(2,1)S(1)} all-to-all(bf16[8,8,1792]{2,1,0:T(8,128)(2,1)S(1)} %fusion), channel_id=1, replica_groups={{0,4,8,12,16,20,24,28},{1,5,9,13,17,21,25,29},{2,6,10,14,18,22,26,30},{..., dimensions={0} | all-to-all | bytes 458752 | tf_op jit(solution)/shard_map/all_to_all | solution.py:27
  92.1 3.4 %all-to-all-start.3 = ((bf16[8,8,1920]{2,1,0:T(8,128)(2,1)}), bf16[8,8,1920]{2,1,0:T(8,128)(2,1)S(1)}, u32[]{:S(2)}, u32[]{:S(2)}) async-start(bf16[8,8,1920]{2,1,0:T(8,128)(2,1)} %copy-done.16), calls=%async_computation.3 | async-start | bytes 491520 | tf_op jit(solution)/shard_map/all_to_all | solution.py:27
  95.6 9.2 %collective-permute-done.13.rest_2_ = bf16[2688,256]{1,0:T(8,128)(2,1)} collective-permute-done((bf16[2688,256]{1,0:T(8,128)(2,1)}, bf16[2688,256]{1,0:T(8,128)(2,1)}, u32[]{:S(2)}, u32[]{:S(2)}) %collective-permute-start.13) | collective-permute-done | bytes 1376288 | tf_op jit(solution)/shard_map/ppermute | solution.py:23
  107.2 2.9 %collective-permute-start.15 = (bf16[64,1920]{1,0:T(8,128)(2,1)S(1)}, bf16[64,1920]{1,0:T(8,128)(2,1)S(1)}, u32[]{:S(2)}, u32[]{:S(2)}) collective-permute-start(bf16[64,1920]{1,0:T(8,128)(2,1)S(1)} %bitcast.44), channel_id=1, source_target_pairs={{0,2},{1,3},{2,0},{3,1},{4,6},{5,7},{6,4},{7,5},{8,10},{9,11},{10,... | collective-permute-start | bytes 737288 | tf_op jit(solution)/shard_map/ppermute | solution.py:563
  110.1 4.8 %collective-permute-done.14.rest_1_ = bf16[64,1920]{1,0:T(8,128)(2,1)S(1)} collective-permute-done((bf16[64,1920]{1,0:T(8,128)(2,1)S(1)}, bf16[64,1920]{1,0:T(8,128)(2,1)S(1)}, u32[]{:S(2)}, u32[]{:S(2)}) %collective-permute-start.14) | collective-permute-done | bytes 245792 | tf_op jit(solution)/shard_map/ppermute | solution.py:563
  114.9 2.2 %collective-permute-done.15.rest_2_ = bf16[64,1920]{1,0:T(8,128)(2,1)S(1)} collective-permute-done((bf16[64,1920]{1,0:T(8,128)(2,1)S(1)}, bf16[64,1920]{1,0:T(8,128)(2,1)S(1)}, u32[]{:S(2)}, u32[]{:S(2)}) %collective-permute-start.15) | collective-permute-done | bytes 245792 | tf_op jit(solution)/shard_map/ppermute | solution.py:563
  117.1 2.6 %collective-permute-done.16.rest_3_ = bf16[64,1920]{1,0:T(8,128)(2,1)S(1)} collective-permute-done((bf16[64,1920]{1,0:T(8,128)(2,1)S(1)}, bf16[64,1920]{1,0:T(8,128)(2,1)S(1)}, u32[]{:S(2)}, u32[]{:S(2)}) %collective-permute-start.16) | collective-permute-done | bytes 245792 | tf_op jit(solution)/shard_map/ppermute | solution.py:563
  122.6 2.5 %shard_map.218 = bf16[4,64,1152]{2,1,0:T(8,128)(2,1)S(1)} custom-call(s32[1]{0:T(128)} %bitcast.at_ref, bf16[128,1920]{1,0:T(8,128)(2,1)S(1)} %shard_map.217.own_ref, bf16[128,1920]{1,0:T(8,128)(2,1)S(1)} %collective-permute-done.17.other_ref, bf16[2688,256]{1,0:T(8,128)(2,1)S(1)} %copy-done.1, bf16[2688,256]{1,0:T(8,128)(2,1)S(1)} %copy-done.3, ...), custom_call_target="tpu_custom_call" | custom-call | tf_op jit(solution)/shard_map/pallas_call | solution.py:436
  125.1 13.1 %all_to_all.37.sums_ref = bf16[4,64,1152]{2,1,0:T(8,128)(2,1)S(1)} all-to-all(bf16[4,64,1152]{2,1,0:T(8,128)(2,1)S(1)} %shard_map.218), channel_id=1, replica_groups=mesh['pd'=2,'dp'=4,'ep'=32] {'dp'}, dimensions={0} | all-to-all | bytes 1179648 | tf_op jit(solution)/shard_map/all_to_all | solution.py:27
  138.5 9.1 %all_to_all.38.acts_ref = bf16[4,64,512]{2,1,0:T(8,128)(2,1)S(1)} all-to-all(bf16[4,64,512]{2,1,0:T(8,128)(2,1)S(1)} %shard_map.219), channel_id=1, replica_groups=mesh['pd'=2,'dp'=4,'ep'=32] {'dp'}, dimensions={0} | all-to-all | bytes 524288 | tf_op jit(solution)/shard_map/all_to_all | solution.py:27
  147.5 4.1 %shard_map.220 = (bf16[128,1792]{1,0:T(8,128)(2,1)S(1)}, bf16[128,1792]{1,0:T(8,128)(2,1)}) custom-call(s32[1]{0:T(128)} %bitcast.at_ref, bf16[4,64,512]{2,1,0:T(8,128)(2,1)S(1)} %all_to_all.38.acts_ref, bf16[2688,256]{1,0:T(8,128)(2,1)S(1)} %copy-done.1, bf16[2688,256]{1,0:T(8,128)(2,1)S(1)} %copy-done.3, ...), custom_call_target="tpu_custom_call" | custom-call | tf_op jit(solution)/shard_map/pallas_call | solution.py:476
  156.6 3.0 %collective-permute-start.20 = (bf16[64,1792]{1,0:T(8,128)(2,1)S(1)}, bf16[64,1792]{1,0:T(8,128)(2,1)S(1)}, u32[]{:S(2)}, u32[]{:S(2)}) collective-permute-start(bf16[64,1792]{1,0:T(8,128)(2,1)S(1)} %get-tuple-element.130), channel_id=1, source_target_pairs={{0,2},{1,3},{2,0},{3,1},{4,6},{5,7},{6,4},{7,5},{8,10},{9,11},{10,... | collective-permute-start | bytes 688136 | tf_op jit(solution)/shard_map/ppermute | solution.py:563
  159.6 4.9 %collective-permute-done.19.rest_1_ = bf16[64,1792]{1,0:T(8,128)(2,1)S(1)} collective-permute-done((bf16[64,1792]{1,0:T(8,128)(2,1)S(1)}, bf16[64,1792]{1,0:T(8,128)(2,1)S(1)}, u32[]{:S(2)}, u32[]{:S(2)}) %collective-permute-start.19) | collective-permute-done | bytes 229408 | tf_op jit(solution)/shard_map/ppermute | solution.py:563
  166.6 3.8 %collective-permute-done.21.rest_3_ = bf16[64,1792]{1,0:T(8,128)(2,1)S(1)} collective-permute-done((bf16[64,1792]{1,0:T(8,128)(2,1)S(1)}, bf16[64,1792]{1,0:T(8,128)(2,1)S(1)}, u32[]{:S(2)}, u32[]{:S(2)}) %collective-permute-start.21) | collective-permute-done | bytes 229408 | tf_op jit(solution)/shard_map/ppermute | solution.py:563
  171.0 20.1 %all_to_all.39 = bf16[32,2,1792]{2,1,0:T(2,128)(2,1)S(1)} all-to-all(bf16[32,2,1792]{2,1,0:T(2,128)(2,1)S(1)} %reshape.32), channel_id=1, replica_groups={{0,4,8,12,16,20,24,28,32,36,40,44,48,52,56,60,64,68,72,76,80,84,88,92,9..., dimensions={0} | all-to-all | bytes 458752 | tf_op jit(solution)/shard_map/all_to_all | solution.py:27
  (123 shorter events, 44.9 us)
Async XLA Ops:
  3.2 7.0 %collective-permute-start = (bf16[80,640]{1,0:T(8,128)(2,1)S(1)}, bf16[80,640]{1,0:T(8,128)(2,1)S(1)}, u32[]{:S(2)}, u32[]{:S(2)}) collective-permute-start(bf16[80,640]{1,0:T(8,128)(2,1)S(1)} %get-tuple-element.67), channel_id=1, source_target_pairs={{0,32},{32,64},{64,96},{96,0},{1,33},{33,65},{65,97},{97,1},{2,34}... | collective-permute-start | bytes 307208 | tf_op jit(solution)/shard_map/ppermute | solution.py:23
  4.7 14.4 %collective-permute-start.3 = (bf16[512,128]{1,0:T(8,128)(2,1)}, bf16[512,128]{1,0:T(8,128)(2,1)}, u32[]{:S(2)}, u32[]{:S(2)}) collective-permute-start(bf16[512,128]{1,0:T(8,128)(2,1)} %bitcast.54), channel_id=1, source_target_pairs={{0,1},{1,2},{2,3},{3,0},{4,5},{5,6},{6,7},{7,4},{8,9},{9,10},{10,1... | collective-permute-start | bytes 393224 | tf_op jit(solution)/shard_map/ppermute | solution.py:563
  5.1 14.0 %collective-permute-start.4 = (bf16[512,128]{1,0:T(8,128)(2,1)}, bf16[512,128]{1,0:T(8,128)(2,1)S(1)}, u32[]{:S(2)}, u32[]{:S(2)}) collective-permute-start(bf16[512,128]{1,0:T(8,128)(2,1)} %bitcast.55), channel_id=1, source_target_pairs={{0,2},{1,3},{2,0},{3,1},{4,6},{5,7},{6,4},{7,5},{8,10},{9,11},{10,... | collective-permute-start | bytes 393224 | tf_op jit(solution)/shard_map/ppermute | solution.py:563
  7.5 11.7 %collective-permute-start.5 = (bf16[512,128]{1,0:T(8,128)(2,1)}, bf16[512,128]{1,0:T(8,128)(2,1)S(1)}, u32[]{:S(2)}, u32[]{:S(2)}) collective-permute-start(bf16[512,128]{1,0:T(8,128)(2,1)} %bitcast.56), channel_id=1, source_target_pairs={{0,3},{1,0},{2,1},{3,2},{4,7},{5,4},{6,5},{7,6},{8,11},{9,8},{10,9... | collective-permute-start | bytes 393224 | tf_op jit(solution)/shard_map/ppermute | solution.py:563
  7.5 11.6 %collective-permute-start.1 = (bf16[80,640]{1,0:T(8,128)(2,1)S(1)}, bf16[80,640]{1,0:T(8,128)(2,1)S(1)}, u32[]{:S(2)}, u32[]{:S(2)}) collective-permute-start(bf16[80,640]{1,0:T(8,128)(2,1)S(1)} %get-tuple-element.70), channel_id=1, source_target_pairs={{0,64},{32,96},{64,0},{96,32},{1,65},{33,97},{65,1},{97,33},{2,66}... | collective-permute-start | bytes 307208 | tf_op jit(solution)/shard_map/ppermute | solution.py:23
  10.2 8.9 %collective-permute-start.2 = (bf16[80,640]{1,0:T(8,128)(2,1)S(1)}, bf16[80,640]{1,0:T(8,128)(2,1)S(1)}, u32[]{:S(2)}, u32[]{:S(2)}) collective-permute-start(bf16[80,640]{1,0:T(8,128)(2,1)S(1)} %get-tuple-element.71), channel_id=1, source_target_pairs={{0,96},{32,0},{64,32},{96,64},{1,97},{33,1},{65,33},{97,65},{2,98}... | collective-permute-start | bytes 307208 | tf_op jit(solution)/shard_map/ppermute | solution.py:23
  19.9 47.7 %collective-permute-start.10 = (bf16[2688,256]{1,0:T(8,128)(2,1)}, bf16[2688,256]{1,0:T(8,128)(2,1)S(1)}, u32[]{:S(2)}, u32[]{:S(2)}) collective-permute-start(bf16[2688,256]{1,0:T(8,128)(2,1)} %get-tuple-element.107), channel_id=1, source_target_pairs={{0,32},{32,64},{64,96},{96,0},{1,33},{33,65},{65,97},{97,1},{2,34}... | collective-permute-start | bytes 4128776 | tf_op jit(solution)/shard_map/ppermute | solution.py:23
  20.4 47.1 %collective-permute-start.11 = (bf16[2688,256]{1,0:T(8,128)(2,1)}, bf16[2688,256]{1,0:T(8,128)(2,1)}, u32[]{:S(2)}, u32[]{:S(2)}) collective-permute-start(bf16[2688,256]{1,0:T(8,128)(2,1)} %get-tuple-element.108), channel_id=1, source_target_pairs={{0,96},{32,0},{64,32},{96,64},{1,97},{33,1},{65,33},{97,65},{2,98}... | collective-permute-start | bytes 4128776 | tf_op jit(solution)/shard_map/ppermute | solution.py:23
  23.9 31.8 %collective-permute-start.6 = (bf16[128,1792]{1,0:T(8,128)(2,1)}, bf16[128,1792]{1,0:T(8,128)(2,1)}, u32[]{:S(2)}, u32[]{:S(2)}) collective-permute-start(bf16[128,1792]{1,0:T(8,128)(2,1)} %constant_dynamic-slice_fusion.2.rest_0_), channel_id=1, source_target_pairs={{0,1},{1,2},{2,3},{3,0},{4,5},{5,6},{6,7},{7,4},{8,9},{9,10},{10,1... | collective-permute-start | bytes 1376264 | tf_op jit(solution)/shard_map/ppermute | solution.py:563
  27.2 28.6 %collective-permute-start.7 = (bf16[128,1792]{1,0:T(8,128)(2,1)}, bf16[128,1792]{1,0:T(8,128)(2,1)}, u32[]{:S(2)}, u32[]{:S(2)}) collective-permute-start(bf16[128,1792]{1,0:T(8,128)(2,1)} %constant_dynamic-slice_fusion.2.rest_0_), channel_id=1, source_target_pairs={{0,3},{1,0},{2,1},{3,2},{4,7},{5,4},{6,5},{7,6},{8,11},{9,8},{10,9... | collective-permute-start | bytes 1376264 | tf_op jit(solution)/shard_map/ppermute | solution.py:563
  27.2 32.0 %collective-permute-start.9 = (bf16[128,1792]{1,0:T(8,128)(2,1)}, bf16[128,1792]{1,0:T(8,128)(2,1)}, u32[]{:S(2)}, u32[]{:S(2)}) collective-permute-start(bf16[128,1792]{1,0:T(8,128)(2,1)} %constant_dynamic-slice_fusion.2.rest_0_), channel_id=1, source_target_pairs={{0,2},{1,3},{2,0},{3,1},{4,6},{5,7},{6,4},{7,5},{8,10},{9,11},{10,... | collective-permute-start | bytes 1376264 | tf_op jit(solution)/shard_map/ppermute | solution.py:563
  34.0 21.8 %all-to-all-start = ((bf16[8,2,8,512]{3,2,1,0:T(8,128)(2,1)}), bf16[8,2,8,512]{3,2,1,0:T(8,128)(2,1)S(1)}, u32[]{:S(2)}, u32[]{:S(2)}) async-start(bf16[8,2,8,512]{3,2,1,0:T(8,128)(2,1)} %shard_map.210), calls=%async_computation | async-start | bytes 262144 | tf_op jit(solution)/shard_map/all_to_all | solution.py:27
  56.5 1.3 collective-permute-start.8
  70.3 1.6 collective-permute-start.12
  70.4 34.4 %collective-permute-start.13 = (bf16[2688,256]{1,0:T(8,128)(2,1)}, bf16[2688,256]{1,0:T(8,128)(2,1)}, u32[]{:S(2)}, u32[]{:S(2)}) collective-permute-start(bf16[2688,256]{1,0:T(8,128)(2,1)} %get-tuple-element.119), channel_id=1, source_target_pairs={{0,64},{32,96},{64,0},{96,32},{1,65},{33,97},{65,1},{97,33},{2,66}... | collective-permute-start | bytes 4128776 | tf_op jit(solution)/shard_map/ppermute | solution.py:23
  92.1 13.9 %all-to-all-start.3 = ((bf16[8,8,1920]{2,1,0:T(8,128)(2,1)}), bf16[8,8,1920]{2,1,0:T(8,128)(2,1)S(1)}, u32[]{:S(2)}, u32[]{:S(2)}) async-start(bf16[8,8,1920]{2,1,0:T(8,128)(2,1)} %copy-done.16), calls=%async_computation.3 | async-start | bytes 491520 | tf_op jit(solution)/shard_map/all_to_all | solution.py:27
  106.1 8.8 %collective-permute-start.14 = (bf16[64,1920]{1,0:T(8,128)(2,1)S(1)}, bf16[64,1920]{1,0:T(8,128)(2,1)S(1)}, u32[]{:S(2)}, u32[]{:S(2)}) collective-permute-start(bf16[64,1920]{1,0:T(8,128)(2,1)S(1)} %bitcast.43), channel_id=1, source_target_pairs={{0,1},{1,2},{2,3},{3,0},{4,5},{5,6},{6,7},{7,4},{8,9},{9,10},{10,1... | collective-permute-start | bytes 737288 | tf_op jit(solution)/shard_map/ppermute | solution.py:563
  107.2 9.9 %collective-permute-start.15 = (bf16[64,1920]{1,0:T(8,128)(2,1)S(1)}, bf16[64,1920]{1,0:T(8,128)(2,1)S(1)}, u32[]{:S(2)}, u32[]{:S(2)}) collective-permute-start(bf16[64,1920]{1,0:T(8,128)(2,1)S(1)} %bitcast.44), channel_id=1, source_target_pairs={{0,2},{1,3},{2,0},{3,1},{4,6},{5,7},{6,4},{7,5},{8,10},{9,11},{10,... | collective-permute-start | bytes 737288 | tf_op jit(solution)/shard_map/ppermute | solution.py:563
  110.1 9.6 %collective-permute-start.16 = (bf16[64,1920]{1,0:T(8,128)(2,1)S(1)}, bf16[64,1920]{1,0:T(8,128)(2,1)S(1)}, u32[]{:S(2)}, u32[]{:S(2)}) collective-permute-start(bf16[64,1920]{1,0:T(8,128)(2,1)S(1)} %bitcast.45), channel_id=1, source_target_pairs={{0,3},{1,0},{2,1},{3,2},{4,7},{5,4},{6,5},{7,6},{8,11},{9,8},{10,9... | collective-permute-start | bytes 737288 | tf_op jit(solution)/shard_map/ppermute | solution.py:563
  120.7 2.0 %collective-permute-start.17 = (bf16[128,1920]{1,0:T(8,128)(2,1)S(1)}, bf16[128,1920]{1,0:T(8,128)(2,1)S(1)}, u32[]{:S(2)}, u32[]{:S(2)}) collective-permute-start(bf16[128,1920]{1,0:T(8,128)(2,1)S(1)} %shard_map.217.own_ref), channel_id=1, source_target_pairs={{0,128},{128,0},{1,129},{129,1},{2,130},{130,2},{3,131},{131,3},{4... | collective-permute-start | bytes 1474568 | tf_op jit(solution)/shard_map/ppermute | solution.py:23
  152.4 2.0 %collective-permute-start.18 = (bf16[128,1792]{1,0:T(8,128)(2,1)}, bf16[128,1792]{1,0:T(8,128)(2,1)S(1)}, u32[]{:S(2)}, u32[]{:S(2)}) collective-permute-start(bf16[128,1792]{1,0:T(8,128)(2,1)} %get-tuple-element.126), channel_id=1, source_target_pairs={{0,128},{128,0},{1,129},{129,1},{2,130},{130,2},{3,131},{131,3},{4... | collective-permute-start | bytes 1376264 | tf_op jit(solution)/shard_map/ppermute | solution.py:23
  156.0 8.5 %collective-permute-start.19 = (bf16[64,1792]{1,0:T(8,128)(2,1)S(1)}, bf16[64,1792]{1,0:T(8,128)(2,1)S(1)}, u32[]{:S(2)}, u32[]{:S(2)}) collective-permute-start(bf16[64,1792]{1,0:T(8,128)(2,1)S(1)} %get-tuple-element.131), channel_id=1, source_target_pairs={{0,1},{1,2},{2,3},{3,0},{4,5},{5,6},{6,7},{7,4},{8,9},{9,10},{10,1... | collective-permute-start | bytes 688136 | tf_op jit(solution)/shard_map/ppermute | solution.py:563
  156.6 10.0 %collective-permute-start.20 = (bf16[64,1792]{1,0:T(8,128)(2,1)S(1)}, bf16[64,1792]{1,0:T(8,128)(2,1)S(1)}, u32[]{:S(2)}, u32[]{:S(2)}) collective-permute-start(bf16[64,1792]{1,0:T(8,128)(2,1)S(1)} %get-tuple-element.130), channel_id=1, source_target_pairs={{0,2},{1,3},{2,0},{3,1},{4,6},{5,7},{6,4},{7,5},{8,10},{9,11},{10,... | collective-permute-start | bytes 688136 | tf_op jit(solution)/shard_map/ppermute | solution.py:563
  159.6 10.8 %collective-permute-start.21 = (bf16[64,1792]{1,0:T(8,128)(2,1)S(1)}, bf16[64,1792]{1,0:T(8,128)(2,1)S(1)}, u32[]{:S(2)}, u32[]{:S(2)}) collective-permute-start(bf16[64,1792]{1,0:T(8,128)(2,1)S(1)} %get-tuple-element.129), channel_id=1, source_target_pairs={{0,3},{1,0},{2,1},{3,2},{4,7},{5,4},{6,5},{7,6},{8,11},{9,8},{10,9... | collective-permute-start | bytes 688136 | tf_op jit(solution)/shard_map/ppermute | solution.py:563
  (34 other events, 255.6 us)
